TPU v7x, 128 devices: a whole 4x4x4 slice. The times are simulated.
128 devices in a mesh: scen: 2 (over x_hi), hour: 16 (over z, y), reg: 4 (over x_lo, core).
Axes of the slice: x: 4 (x_hi: 2, x_lo: 2; x = x_hi * 2 + x_lo), y: 4, z: 4, core: 2. Of those that a mesh axis runs over, the one named last changes fastest.
Arguments:
- cost_rate: float32 [8, 2688, 2048], P('scen', 'hour', 'reg'), may hold values from 0.05 to 1
- invest_cost: float32 [3, 2048], P(None, 'reg'), may hold values from 0.1 to 1
- tile: bfloat16 [16, 256, 2048], P('hour', None, 'reg'), may hold values from -0.1875 to 0.1875
- tile_mask: int32 [16, 256, 2048], P('hour', None, 'reg'), may hold values 0 or 1
- demand: float32 [8, 2688, 256], P('scen', 'hour'), may hold values from -6 to 6
- dispatch: float32 [8, 2688, 2048], P('scen', 'hour', 'reg'), may hold values from 0 to 1
- dual: float32 [8, 2688, 256], P('scen', 'hour'), may hold values from 0 to 1
- cap_dual: float32 [8, 2688, 2048], P('scen', 'hour', 'reg'), may hold values from 0 to 1
- capacity: float32 [8, 3, 2048], P('scen', None, 'reg'), may hold values from 0 to 2
- multiplier: float32 [8, 3, 2048], P('scen', None, 'reg'), may hold values from -3 to 3
- consensus: float32 [8, 3, 2048], P('scen', None, 'reg'), may hold values from 0 to 2
- scen_weight: float32 [8], P('scen'), may hold values from 0.1 to 1
- node_of: int32 [3, 8], P(None, 'scen'), may hold values from 0 to 3, as said below
Outputs:
- dispatch_out: float32 [8, 2688, 2048], P('scen', 'hour', 'reg')
- dual_out: float32 [8, 2688, 256], P('scen', 'hour', 'reg')
- capacity_out: float32 [8, 3, 2048], P('scen', None, 'reg')
- multiplier_out: float32 [8, 3, 2048], P('scen', None, 'reg')
Inputs may be any that keep to these rules, and one draw needn't show every extreme that they name: `node_of`: at each section the nodes are runs of consecutive scenarios, numbered in order from 0; each node of a section lies within one node of the section before; section 0 is one node, the last section has 4 nodes, and node counts grow from section to section.
All inputs are finite; a program needn't handle non-finite values. No bound on the sum of `tile_mask` on one device may be relied on, other than what follows from the above.
Results may differ from a plain program's by a relative error of at most 0.0015.
Values may be sent and summed in bfloat16 or wider, within the bound.
A program may use at most 64 MiB of HBM per device.

v0:
```python
import jax
import jax.numpy as jnp
from jax import lax
from jax.sharding import PartitionSpec as P

ITERS = 8


RAMP_WEIGHT = 0.5
PENALTY = 1.0
STEP_PRIMAL = 0.3
STEP_INVEST = 0.5
STEP_DUAL = 0.3
STEP_CAP = 0.05


def with_halo(cells, sides, width):
    for axis, dim in sides:
        count = lax.axis_size(axis)
        ends = count - 1
        head = lax.slice_in_dim(cells, 0, width, axis=dim)
        tail = lax.slice_in_dim(cells, cells.shape[dim] - width, cells.shape[dim], axis=dim)
        cells = jnp.concatenate(
            [
                lax.ppermute(tail, axis, [(i, (i + 1) % count) for i in range(ends)]),
                cells,
                lax.ppermute(head, axis, [((i + 1) % count, i) for i in range(ends)]),
            ],
            axis=dim,
        )
    return cells


def safe_average(node_sum, node_mass):
    safe_mass = node_mass + (node_mass <= 0.0).astype(jnp.float32)
    return node_sum / safe_mass[:, :, None]


def shards(
    cost_rate,
    invest_cost,
    tile,
    tile_mask,
    demand,
    dispatch,
    dual,
    cap_dual,
    capacity,
    multiplier,
    consensus,
    scen_weight,
    node_of,
):
    matrix = tile[0] * tile_mask[0].astype(jnp.bfloat16)
    hours_all = dispatch.shape[1] * lax.axis_size("hour")
    reg_count = lax.axis_size("reg")
    reg_place = lax.axis_index("reg")
    cons_part = dual.shape[2] // reg_count
    first_row = reg_place * cons_part
    primal = dispatch
    cap_var = cap_dual
    invest = capacity
    dual_low = dual.astype(jnp.bfloat16)
    dual_var = dual
    for step_index in range(ITERS):
        padded = with_halo(primal, (("hour", 1),), 1)
        rough = 2.0 * primal - padded[:, :-2] - padded[:, 2:]
        pulled = jnp.einsum("shr,rc->shc", dual_low, matrix, preferred_element_type=jnp.float32)
        grad_x = cost_rate + RAMP_WEIGHT * rough - pulled + cap_var
        zmean = lax.psum(jnp.sum(cap_var, axis=1), "hour") / hours_all
        grad_u = invest_cost[None] + multiplier + PENALTY * (invest - consensus) - zmean[:, None, :]
        primal_new = jnp.maximum(primal - STEP_PRIMAL * grad_x, 0.0)
        invest_new = jnp.maximum(invest - STEP_INVEST * grad_u, 0.0)
        primal_ext = 2.0 * primal_new - primal
        invest_ext = 2.0 * invest_new - invest
        partial_rows = jnp.einsum(
            "shc,rc->shr",
            primal_ext.astype(jnp.bfloat16),
            matrix,
            preferred_element_type=jnp.float32,
        )
        image = lax.psum(partial_rows, "reg")
        dual_var = jnp.maximum(dual_var + STEP_DUAL * (demand - image), 0.0)
        dual_low = dual_var.astype(jnp.bfloat16)
        cap_var = jnp.maximum(
            cap_var + STEP_CAP * (primal_ext - jnp.sum(invest_ext, axis=1)[:, None, :]), 0.0
        )
        primal = primal_new
        invest = invest_new
    dual_out = lax.dynamic_slice_in_dim(dual_var, first_row, cons_part, 2)
    node_count = node_of.shape[1] * lax.axis_size("scen") // 2
    node_ids = jnp.arange(node_count, dtype=jnp.int32)
    one_hot = (node_of[:, :, None] == node_ids[None, None, :]).astype(jnp.float32)
    weighted = scen_weight[:, None, None] * invest
    node_sum = jnp.einsum("gsn,sgc->gnc", one_hot, weighted, precision=lax.Precision.HIGHEST)
    node_mass = jnp.einsum("gsn,s->gn", one_hot, scen_weight, precision=lax.Precision.HIGHEST)
    sum_total, mass_total = lax.psum((node_sum, node_mass), "scen")
    average = safe_average(sum_total, mass_total)
    spread_back = jnp.einsum("gsn,gnc->sgc", one_hot, average, precision=lax.Precision.HIGHEST)
    multiplier_out = multiplier + PENALTY * (invest - spread_back)
    return (primal, dual_out, invest, multiplier_out)


def solution(mesh):
    placed = (
        P("scen", "hour", "reg"),
        P(None, "reg"),
        P("hour", None, "reg"),
        P("hour", None, "reg"),
        P("scen", "hour", None),
        P("scen", "hour", "reg"),
        P("scen", "hour", None),
        P("scen", "hour", "reg"),
        P("scen", None, "reg"),
        P("scen", None, "reg"),
        P("scen", None, "reg"),
        P("scen"),
        P(None, "scen"),
    )
    return jax.shard_map(
        shards,
        mesh=mesh,
        in_specs=placed,
        out_specs=(
            P("scen", "hour", "reg"),
            P("scen", "hour", "reg"),
            P("scen", None, "reg"),
            P("scen", None, "reg"),
        ),
        check_vma=False,
    )
```

profile of v0, /device:TPU:1, one launch (start us, length us, event | category | flops | bytes accessed | tf_op | source)
XLA Modules:
  0.0 458.1 jit_solution(8639232075780562060)
XLA Ops:
  7.3 1.0 fusion.177
  8.3 4.0 collective-permute-start
  12.4 1.3 collective-permute-start.1
  13.7 1.5 reduce_sum.135
  15.1 36.1 %psum.127 = f32[4,512]{1,0:T(4,128)S(1)} all-reduce(f32[4,512]{1,0:T(4,128)S(1)} %reduce_sum.135), channel_id=1, replica_groups=mesh['scen'=2,'hour'=16,'reg'=4] {'hour'}, use_global_device_ids=true, to_apply=%region_2.0 | all-reduce | flops 2048 | bytes 16384 | tf_op jit(solution)/shard_map/psum | solution.py:70
  51.3 1.1 convert_multiply_fusion
  52.5 5.1 %fusion.169 = (f32[4,512]{1,0:T(4,128)S(1)}, f32[4,168,512]{2,1,0:T(8,128)}, f32[4,168,512]{2,1,0:T(8,128)S(1)}) fusion(f32[4,168,512]{2,1,0:T(8,128)} %param.20, f32[4,512]{1,0:T(4,128)S(1)} %get-tuple-element.22, f32[4,168,512]{2,1,0:T(8,128)} %param.18, f32[4,168,256]{2,1,0:T(8,128)S(1)} %copy-done.20, ...), kind=kOutput, calls=%fused_computation.223 | convolution fusion | flops 182867968 | bytes 7864320 | tf_op jit(solution)/shard_map/shr,rc->shc/dot_general | solution.py:68
  57.6 1.1 copy-done.11
  58.7 1.3 fusion.87
  60.1 0.9 fusion.176
  61.0 1.3 collective-permute-start.2
  62.3 1.3 collective-permute-start.3
  63.6 31.5 %psum.129 = f32[4,512]{1,0:T(4,128)S(1)} all-reduce(f32[4,512]{1,0:T(4,128)S(1)} %get-tuple-element.20), channel_id=1, replica_groups=mesh['scen'=2,'hour'=16,'reg'=4] {'hour'}, use_global_device_ids=true, to_apply=%region_6.0 | all-reduce | flops 2048 | bytes 16384 | tf_op jit(solution)/shard_map/psum | solution.py:70
  95.1 8.0 %all-reduce.10.cloned.1.call-done = f32[4,168,256]{2,1,0:T(8,128)} async-done(((f32[4,168,256]{2,1,0:T(8,128)}), f32[4,168,256]{2,1,0:T(8,128)}) %all-reduce.10.cloned.1.call-update) | async-done | bytes 688144 | tf_op jit(solution)/shard_map/psum | solution.py:82
  103.2 5.2 %fusion.168 = (f32[4,512]{1,0:T(4,128)S(1)}, f32[4,168,512]{2,1,0:T(8,128)}, f32[4,168,512]{2,1,0:T(8,128)S(1)}) fusion(f32[4,168,512]{2,1,0:T(8,128)} %get-tuple-element.21, f32[4,512]{1,0:T(4,128)S(1)} %subtract_reduce_fusion.5, f32[4,168,512]{2,1,0:T(8,128)} %copy-done.11, bf16[1,256,512]{2,1,0:T(8,128)(2,1)S(1)} %convert_multiply_fusion, ...), kind=kOutput, calls=%fused_computation.222 | convolution fusion | flops 183556096 | bytes 9240576 | tf_op jit(solution)/shard_map/shr,rc->shc/dot_general | solution.py:68
  108.4 1.1 copy-done.5
  109.5 1.3 fusion.85
  111.7 3.1 collective-permute-start.4
  114.8 1.3 collective-permute-start.5
  116.1 35.6 %psum.131 = f32[4,512]{1,0:T(4,128)S(1)} all-reduce(f32[4,512]{1,0:T(4,128)S(1)} %get-tuple-element.18), channel_id=1, replica_groups=mesh['scen'=2,'hour'=16,'reg'=4] {'hour'}, use_global_device_ids=true, to_apply=%region_10.0 | all-reduce | flops 2048 | bytes 16384 | tf_op jit(solution)/shard_map/psum | solution.py:70
  151.8 1.6 all-reduce.12.cloned.1.call-done
  153.4 1.9 add_maximum_fusion.12
  155.8 2.2 fusion.167
  158.0 1.1 copy-done.7
  159.1 1.3 fusion.83
  161.3 3.1 collective-permute-start.6
  164.4 1.3 collective-permute-start.7
  165.7 36.0 %psum.133 = f32[4,512]{1,0:T(4,128)S(1)} all-reduce(f32[4,512]{1,0:T(4,128)S(1)} %get-tuple-element.16), channel_id=1, replica_groups=mesh['scen'=2,'hour'=16,'reg'=4] {'hour'}, use_global_device_ids=true, to_apply=%region_14.0 | all-reduce | flops 2048 | bytes 16384 | tf_op jit(solution)/shard_map/psum | solution.py:70
  201.8 1.1 all-reduce.14.cloned.1.call-done
  202.9 5.2 %fusion.166 = (f32[4,512]{1,0:T(4,128)S(1)}, f32[4,168,512]{2,1,0:T(8,128)}, f32[4,168,512]{2,1,0:T(8,128)S(1)}) fusion(f32[4,168,512]{2,1,0:T(8,128)} %get-tuple-element.17, f32[4,512]{1,0:T(4,128)S(1)} %subtract_reduce_fusion.3, f32[4,168,512]{2,1,0:T(8,128)} %copy-done.7, bf16[1,256,512]{2,1,0:T(8,128)(2,1)S(1)} %convert_multiply_fusion, ...), kind=kOutput, calls=%fused_computation.220 | convolution fusion | flops 183556096 | bytes 9240576 | tf_op jit(solution)/shard_map/shr,rc->shc/dot_general | solution.py:68
  208.2 1.1 copy-done.3
  209.2 1.3 fusion.81
  211.5 3.1 collective-permute-start.8
  214.5 1.3 collective-permute-start.9
  215.8 35.3 %psum.135 = f32[4,512]{1,0:T(4,128)S(1)} all-reduce(f32[4,512]{1,0:T(4,128)S(1)} %get-tuple-element.14), channel_id=1, replica_groups=mesh['scen'=2,'hour'=16,'reg'=4] {'hour'}, use_global_device_ids=true, to_apply=%region_18.0 | all-reduce | flops 2048 | bytes 16384 | tf_op jit(solution)/shard_map/psum | solution.py:70
  251.3 1.9 all-reduce.16.cloned.1.call-done
  253.2 1.6 add_maximum_fusion.10
  255.3 2.2 fusion.165
  257.5 1.1 copy-done.9
  258.6 1.3 fusion.79
  260.9 3.1 collective-permute-start.10
  263.9 1.3 collective-permute-start.11
  265.2 35.5 %psum.137 = f32[4,512]{1,0:T(4,128)S(1)} all-reduce(f32[4,512]{1,0:T(4,128)S(1)} %get-tuple-element.12), channel_id=1, replica_groups=mesh['scen'=2,'hour'=16,'reg'=4] {'hour'}, use_global_device_ids=true, to_apply=%region_22.0 | all-reduce | flops 2048 | bytes 16384 | tf_op jit(solution)/shard_map/psum | solution.py:70
  300.9 1.9 all-reduce.18.cloned.1.call-done
  302.8 5.5 %fusion.164 = (f32[4,512]{1,0:T(4,128)S(1)}, f32[4,168,512]{2,1,0:T(8,128)}, f32[4,168,512]{2,1,0:T(8,128)S(1)}) fusion(f32[4,168,512]{2,1,0:T(8,128)} %get-tuple-element.13, f32[4,512]{1,0:T(4,128)S(1)} %subtract_reduce_fusion.1, f32[4,168,512]{2,1,0:T(8,128)} %copy-done.9, bf16[1,256,512]{2,1,0:T(8,128)(2,1)S(1)} %convert_multiply_fusion, ...), kind=kOutput, calls=%fused_computation.218 | convolution fusion | flops 183556096 | bytes 9240576 | tf_op jit(solution)/shard_map/shr,rc->shc/dot_general | solution.py:68
  308.3 1.3 fusion.77
  309.7 3.1 collective-permute-start.12
  312.8 1.3 collective-permute-start.13
  314.1 35.3 %psum.139 = f32[4,512]{1,0:T(4,128)S(1)} all-reduce(f32[4,512]{1,0:T(4,128)S(1)} %get-tuple-element.10), channel_id=1, replica_groups=mesh['scen'=2,'hour'=16,'reg'=4] {'hour'}, use_global_device_ids=true, to_apply=%region_26.0 | all-reduce | flops 2048 | bytes 16384 | tf_op jit(solution)/shard_map/psum | solution.py:70
  349.6 2.7 all-reduce.20.cloned.1.call-done
  352.3 3.4 fusion.139
  355.7 1.1 copy-done.13
  356.8 1.3 fusion.75
  358.4 0.9 fusion.170
  359.2 3.2 collective-permute-start.14
  362.5 1.3 collective-permute-start.15
  363.8 35.2 %psum.141 = f32[4,512]{1,0:T(4,128)S(1)} all-reduce(f32[4,512]{1,0:T(4,128)S(1)} %get-tuple-element.46), channel_id=1, replica_groups=mesh['scen'=2,'hour'=16,'reg'=4] {'hour'}, use_global_device_ids=true, to_apply=%region_30.0 | all-reduce | flops 2048 | bytes 16384 | tf_op jit(solution)/shard_map/psum | solution.py:70
  400.0 1.9 add_maximum_fusion.7
  402.7 1.0 fusion.7
  403.8 1.1 copy-done.18
  404.8 1.3 fusion.74
  406.4 9.4 %all-reduce = (f32[3,4,512]{2,1,0:T(4,128)S(1)}, f32[3,4]{1,0:T(4,128)S(1)}) all-reduce(f32[3,4,512]{2,1,0:T(4,128)S(1)} %fusion.140, f32[3,4]{1,0:T(4,128)S(1)} %bitcast.64), channel_id=1, replica_groups=mesh['scen'=2,'hour'=16,'reg'=4] {'scen'}, use_global_device_ids=true, to_apply=%region_31.0 | all-reduce | flops 6156 | bytes 49248 | tf_op jit(solution)/shard_map/psum | solution.py:97
  416.7 32.3 %all-reduce.24.cloned.1.call-done = f32[4,168,256]{2,1,0:T(8,128)} async-done(((f32[4,168,256]{2,1,0:T(8,128)}), f32[4,168,256]{2,1,0:T(8,128)}) %all-reduce.24.cloned.1.call-update) | async-done | bytes 688144 | tf_op jit(solution)/shard_map/psum | solution.py:82
  449.0 1.4 fusion.90
  (117 shorter events, 9.7 us)
Async XLA Ops:
  7.2 44.1 %copy-start.26 = (bf16[1,256,512]{2,1,0:T(8,128)(2,1)S(1)}, bf16[1,256,512]{2,1,0:T(8,128)(2,1)}, u32[]{:S(2)}) copy-start(bf16[1,256,512]{2,1,0:T(8,128)(2,1)} %param.15) | copy-start | bytes 786436
  7.2 45.2 %copy-start.29 = (f32[3,512]{1,0:T(4,128)S(1)}, f32[3,512]{1,0:T(4,128)}, u32[]{:S(2)}) copy-start(f32[3,512]{1,0:T(4,128)} %param.14) | copy-start | bytes 18436
  7.2 45.2 %copy-start.21 = (f32[4,3,512]{2,0,1:T(4,128)S(1)}, f32[4,3,512]{2,0,1:T(4,128)}, u32[]{:S(2)}) copy-start(f32[4,3,512]{2,0,1:T(4,128)} %param.21) | copy-start | bytes 73732
  7.2 45.2 %copy-start.28 = (f32[4,3,512]{2,0,1:T(4,128)S(1)}, f32[4,3,512]{2,0,1:T(4,128)}, u32[]{:S(2)}) copy-start(f32[4,3,512]{2,0,1:T(4,128)} %param.22) | copy-start | bytes 73732
  7.2 45.2 %copy-start.22 = (f32[4,3,512]{2,0,1:T(4,128)S(1)}, f32[4,3,512]{2,0,1:T(4,128)}, u32[]{:S(2)}) copy-start(f32[4,3,512]{2,0,1:T(4,128)} %param.23) | copy-start | bytes 73732
  7.2 45.2 %copy-start.1 = (f32[4,168,512]{2,1,0:T(8,128)S(1)}, f32[4,168,512]{2,1,0:T(8,128)}, u32[]{:S(2)}) copy-start(f32[4,168,512]{2,1,0:T(8,128)} %param.13) | copy-start | bytes 4128772
  7.2 45.2 %copy-start.20 = (f32[4,168,256]{2,1,0:T(8,128)S(1)}, f32[4,168,256]{2,1,0:T(8,128)}, u32[]{:S(2)}) copy-start(f32[4,168,256]{2,1,0:T(8,128)} %param.19) | copy-start | bytes 2064388
  7.2 95.9 %all-reduce.10.cloned.1.call-start = ((), (), s32[]{:S(2)}) async-start(), calls=%async_computation | async-start | bytes 1376256 | tf_op jit(solution)/shard_map/psum | solution.py:82
  8.3 44.1 %collective-permute-start = (f32[4,1,512]{2,1,0:T(1,128)S(1)}, f32[4,1,512]{2,1,0:T(1,128)S(1)}, u32[]{:S(2)}, u32[]{:S(2)}) collective-permute-start(f32[4,1,512]{2,1,0:T(1,128)S(1)} %get-tuple-element.38), channel_id=1, source_target_pairs={{0,4},{4,8},{8,12},{12,16},{16,20},{20,24},{24,28},{28,32},{32,36}... | collective-permute-start | bytes 24584 | tf_op jit(solution)/shard_map/ppermute | solution.py:25
  12.4 40.1 %collective-permute-start.1 = (f32[4,1,512]{2,1,0:T(1,128)S(1)}, f32[4,1,512]{2,1,0:T(1,128)S(1)}, u32[]{:S(2)}, u32[]{:S(2)}) collective-permute-start(f32[4,1,512]{2,1,0:T(1,128)S(1)} %get-tuple-element.39), channel_id=1, source_target_pairs={{4,0},{8,4},{12,8},{16,12},{20,16},{24,20},{28,24},{32,28},{36,32}... | collective-permute-start | bytes 24584 | tf_op jit(solution)/shard_map/ppermute | solution.py:27
  52.5 6.3 %copy-start.23 = (f32[4,168,512]{2,1,0:T(8,128)S(1)}, f32[4,168,512]{2,1,0:T(8,128)}, u32[]{:S(2)}) copy-start(f32[4,168,512]{2,1,0:T(8,128)} %param.18) | copy-start | bytes 4128772
  57.6 1.1 copy-start.11
  58.7 44.4 %copy-start = (f32[4,168,256]{2,1,0:T(8,128)S(1)}, f32[4,168,256]{2,1,0:T(8,128)}, u32[]{:S(2)}) copy-start(f32[4,168,256]{2,1,0:T(8,128)} %param.17) | copy-start | bytes 2064388
  60.0 93.4 %all-reduce.12.cloned.1.call-start = ((), (), s32[]{:S(2)}) async-start(), calls=%async_computation.1 | async-start | bytes 1376256 | tf_op jit(solution)/shard_map/psum | solution.py:82
  61.0 34.1 %collective-permute-start.2 = (f32[4,1,512]{2,1,0:T(1,128)S(1)}, f32[4,1,512]{2,1,0:T(1,128)S(1)}, u32[]{:S(2)}, u32[]{:S(2)}) collective-permute-start(f32[4,1,512]{2,1,0:T(1,128)S(1)} %get-tuple-element.36), channel_id=1, source_target_pairs={{0,4},{4,8},{8,12},{12,16},{16,20},{20,24},{24,28},{28,32},{32,36}... | collective-permute-start | bytes 24584 | tf_op jit(solution)/shard_map/ppermute | solution.py:25
  62.3 32.8 %collective-permute-start.3 = (f32[4,1,512]{2,1,0:T(1,128)S(1)}, f32[4,1,512]{2,1,0:T(1,128)S(1)}, u32[]{:S(2)}, u32[]{:S(2)}) collective-permute-start(f32[4,1,512]{2,1,0:T(1,128)S(1)} %get-tuple-element.37), channel_id=1, source_target_pairs={{4,0},{8,4},{12,8},{16,12},{20,16},{24,20},{28,24},{32,28},{36,32}... | collective-permute-start | bytes 24584 | tf_op jit(solution)/shard_map/ppermute | solution.py:27
  103.2 6.3 %copy-start.12 = (f32[4,168,512]{2,1,0:T(8,128)S(1)}, f32[4,168,512]{2,1,0:T(8,128)}, u32[]{:S(2)}) copy-start(f32[4,168,512]{2,1,0:T(8,128)} %copy-done.11) | copy-start | bytes 4128772
  108.4 1.1 copy-start.5
  110.8 92.1 %all-reduce.14.cloned.1.call-start = ((), (), s32[]{:S(2)}) async-start(), calls=%async_computation.2 | async-start | bytes 1376256 | tf_op jit(solution)/shard_map/psum | solution.py:82
  111.7 43.5 %collective-permute-start.4 = (f32[4,1,512]{2,1,0:T(1,128)S(1)}, f32[4,1,512]{2,1,0:T(1,128)S(1)}, u32[]{:S(2)}, u32[]{:S(2)}) collective-permute-start(f32[4,1,512]{2,1,0:T(1,128)S(1)} %get-tuple-element.34), channel_id=1, source_target_pairs={{0,4},{4,8},{8,12},{12,16},{16,20},{20,24},{24,28},{28,32},{32,36}... | collective-permute-start | bytes 24584 | tf_op jit(solution)/shard_map/ppermute | solution.py:25
  114.8 40.5 %collective-permute-start.5 = (f32[4,1,512]{2,1,0:T(1,128)S(1)}, f32[4,1,512]{2,1,0:T(1,128)S(1)}, u32[]{:S(2)}, u32[]{:S(2)}) collective-permute-start(f32[4,1,512]{2,1,0:T(1,128)S(1)} %get-tuple-element.35), channel_id=1, source_target_pairs={{4,0},{8,4},{12,8},{16,12},{20,16},{24,20},{28,24},{32,28},{36,32}... | collective-permute-start | bytes 24584 | tf_op jit(solution)/shard_map/ppermute | solution.py:27
  153.4 2.0 copy-start.6
  153.4 2.4 copy-start.25
  158.0 1.1 copy-start.7
  160.4 92.8 %all-reduce.16.cloned.1.call-start = ((), (), s32[]{:S(2)}) async-start(), calls=%async_computation.3 | async-start | bytes 1376256 | tf_op jit(solution)/shard_map/psum | solution.py:82
  161.3 40.5 %collective-permute-start.6 = (f32[4,1,512]{2,1,0:T(1,128)S(1)}, f32[4,1,512]{2,1,0:T(1,128)S(1)}, u32[]{:S(2)}, u32[]{:S(2)}) collective-permute-start(f32[4,1,512]{2,1,0:T(1,128)S(1)} %get-tuple-element.32), channel_id=1, source_target_pairs={{0,4},{4,8},{8,12},{12,16},{16,20},{20,24},{24,28},{28,32},{32,36}... | collective-permute-start | bytes 24584 | tf_op jit(solution)/shard_map/ppermute | solution.py:25
  164.4 37.4 %collective-permute-start.7 = (f32[4,1,512]{2,1,0:T(1,128)S(1)}, f32[4,1,512]{2,1,0:T(1,128)S(1)}, u32[]{:S(2)}, u32[]{:S(2)}) collective-permute-start(f32[4,1,512]{2,1,0:T(1,128)S(1)} %get-tuple-element.33), channel_id=1, source_target_pairs={{4,0},{8,4},{12,8},{16,12},{20,16},{24,20},{28,24},{32,28},{36,32}... | collective-permute-start | bytes 24584 | tf_op jit(solution)/shard_map/ppermute | solution.py:27
  202.9 6.3 %copy-start.8 = (f32[4,168,512]{2,1,0:T(8,128)S(1)}, f32[4,168,512]{2,1,0:T(8,128)}, u32[]{:S(2)}) copy-start(f32[4,168,512]{2,1,0:T(8,128)} %copy-done.7) | copy-start | bytes 4128772
  208.2 1.1 copy-start.3
  210.5 92.2 %all-reduce.18.cloned.1.call-start = ((), (), s32[]{:S(2)}) async-start(), calls=%async_computation.4 | async-start | bytes 1376256 | tf_op jit(solution)/shard_map/psum | solution.py:82
  211.5 43.4 %collective-permute-start.8 = (f32[4,1,512]{2,1,0:T(1,128)S(1)}, f32[4,1,512]{2,1,0:T(1,128)S(1)}, u32[]{:S(2)}, u32[]{:S(2)}) collective-permute-start(f32[4,1,512]{2,1,0:T(1,128)S(1)} %get-tuple-element.30), channel_id=1, source_target_pairs={{0,4},{4,8},{8,12},{12,16},{16,20},{20,24},{24,28},{28,32},{32,36}... | collective-permute-start | bytes 24584 | tf_op jit(solution)/shard_map/ppermute | solution.py:25
  214.5 40.3 %collective-permute-start.9 = (f32[4,1,512]{2,1,0:T(1,128)S(1)}, f32[4,1,512]{2,1,0:T(1,128)S(1)}, u32[]{:S(2)}, u32[]{:S(2)}) collective-permute-start(f32[4,1,512]{2,1,0:T(1,128)S(1)} %get-tuple-element.31), channel_id=1, source_target_pairs={{4,0},{8,4},{12,8},{16,12},{20,16},{24,20},{28,24},{32,28},{36,32}... | collective-permute-start | bytes 24584 | tf_op jit(solution)/shard_map/ppermute | solution.py:27
  253.2 1.8 copy-start.4
  253.2 2.2 copy-start.24
  254.8 2.7 copy-start.15
  257.5 1.1 copy-start.9
  258.6 44.1 %copy-start.16 = (f32[4,168,256]{2,1,0:T(8,128)S(1)}, f32[4,168,256]{2,1,0:T(8,128)}, u32[]{:S(2)}) copy-start(f32[4,168,256]{2,1,0:T(8,128)} %copy-done.15) | copy-start | bytes 2064388
  259.9 92.4 %all-reduce.20.cloned.1.call-start = ((), (), s32[]{:S(2)}) async-start(), calls=%async_computation.5 | async-start | bytes 1376256 | tf_op jit(solution)/shard_map/psum | solution.py:82
  260.9 40.0 %collective-permute-start.10 = (f32[4,1,512]{2,1,0:T(1,128)S(1)}, f32[4,1,512]{2,1,0:T(1,128)S(1)}, u32[]{:S(2)}, u32[]{:S(2)}) collective-permute-start(f32[4,1,512]{2,1,0:T(1,128)S(1)} %get-tuple-element.28), channel_id=1, source_target_pairs={{0,4},{4,8},{8,12},{12,16},{16,20},{20,24},{24,28},{28,32},{32,36}... | collective-permute-start | bytes 24584 | tf_op jit(solution)/shard_map/ppermute | solution.py:25
  263.9 36.9 %collective-permute-start.11 = (f32[4,1,512]{2,1,0:T(1,128)S(1)}, f32[4,1,512]{2,1,0:T(1,128)S(1)}, u32[]{:S(2)}, u32[]{:S(2)}) collective-permute-start(f32[4,1,512]{2,1,0:T(1,128)S(1)} %get-tuple-element.29), channel_id=1, source_target_pairs={{4,0},{8,4},{12,8},{16,12},{20,16},{24,20},{28,24},{32,28},{36,32}... | collective-permute-start | bytes 24584 | tf_op jit(solution)/shard_map/ppermute | solution.py:27
  302.8 5.5 %copy-start.10 = (f32[4,168,512]{2,1,0:T(8,128)S(1)}, f32[4,168,512]{2,1,0:T(8,128)}, u32[]{:S(2)}) copy-start(f32[4,168,512]{2,1,0:T(8,128)} %copy-done.9) | copy-start | bytes 4128772
  309.6 90.3 %all-reduce.22.cloned.1.call-start = ((), (), s32[]{:S(2)}) async-start(), calls=%async_computation.6 | async-start | bytes 1376256 | tf_op jit(solution)/shard_map/psum | solution.py:82
  309.7 39.8 %collective-permute-start.12 = (f32[4,1,512]{2,1,0:T(1,128)S(1)}, f32[4,1,512]{2,1,0:T(1,128)S(1)}, u32[]{:S(2)}, u32[]{:S(2)}) collective-permute-start(f32[4,1,512]{2,1,0:T(1,128)S(1)} %get-tuple-element.26), channel_id=1, source_target_pairs={{0,4},{4,8},{8,12},{12,16},{16,20},{20,24},{24,28},{28,32},{32,36}... | collective-permute-start | bytes 24584 | tf_op jit(solution)/shard_map/ppermute | solution.py:25
  312.8 36.8 %collective-permute-start.13 = (f32[4,1,512]{2,1,0:T(1,128)S(1)}, f32[4,1,512]{2,1,0:T(1,128)S(1)}, u32[]{:S(2)}, u32[]{:S(2)}) collective-permute-start(f32[4,1,512]{2,1,0:T(1,128)S(1)} %get-tuple-element.27), channel_id=1, source_target_pairs={{4,0},{8,4},{12,8},{16,12},{20,16},{24,20},{28,24},{32,28},{36,32}... | collective-permute-start | bytes 24584 | tf_op jit(solution)/shard_map/ppermute | solution.py:27
  355.7 1.1 copy-start.13
  356.8 1.4 copy-start.30
  356.8 1.4 copy-start.31
  358.1 90.9 %all-reduce.24.cloned.1.call-start = ((), (), s32[]{:S(2)}) async-start(), calls=%async_computation.7 | async-start | bytes 1376256 | tf_op jit(solution)/shard_map/psum | solution.py:82
  359.2 42.7 %collective-permute-start.14 = (f32[4,1,512]{2,1,0:T(1,128)S(1)}, f32[4,1,512]{2,1,0:T(1,128)S(1)}, u32[]{:S(2)}, u32[]{:S(2)}) collective-permute-start(f32[4,1,512]{2,1,0:T(1,128)S(1)} %get-tuple-element.24), channel_id=1, source_target_pairs={{0,4},{4,8},{8,12},{12,16},{16,20},{20,24},{24,28},{28,32},{32,36}... | collective-permute-start | bytes 24584 | tf_op jit(solution)/shard_map/ppermute | solution.py:25
  362.5 39.4 %collective-permute-start.15 = (f32[4,1,512]{2,1,0:T(1,128)S(1)}, f32[4,1,512]{2,1,0:T(1,128)S(1)}, u32[]{:S(2)}, u32[]{:S(2)}) collective-permute-start(f32[4,1,512]{2,1,0:T(1,128)S(1)} %get-tuple-element.25), channel_id=1, source_target_pairs={{4,0},{8,4},{12,8},{16,12},{20,16},{24,20},{28,24},{32,28},{36,32}... | collective-permute-start | bytes 24584 | tf_op jit(solution)/shard_map/ppermute | solution.py:27
  399.1 16.7 %copy-start.27 = (f32[4,3,512]{2,0,1:T(4,128)}, f32[4,3,512]{2,0,1:T(4,128)S(1)}, u32[]{:S(2)}) copy-start(f32[4,3,512]{2,0,1:T(4,128)S(1)} %subtract_maximum_fusion) | copy-start | bytes 73732
  399.9 2.0 copy-start.2
  399.9 2.4 copy-start.14
  399.9 2.8 copy-start.17
  401.9 1.9 copy-start.19
  403.8 1.1 copy-start.18
Sparse Core Ops, SparseCore 0:
  60.2 42.9 all-reduce.9
  110.9 42.4 all-reduce.11
  160.5 42.3 all-reduce.13
  210.6 42.4 all-reduce.15
  260.0 42.6 all-reduce.17
  309.7 42.4 all-reduce.19
  358.2 41.6 all-reduce.21
  406.3 42.6 all-reduce.23
where the time goes:
time: 459 us; the launch traced here: 458 us
  blocking collectives  290 us (63%)
  waiting for transfers between devices  50.6 us (11%)
  matrix products  41.5 us (9%)
  starting transfers between devices  34.5 us (8%)
  local copies, waits for them, and re-layouts  16.7 us (4%)
  between operations  14.8 us (3%)
  other arithmetic  10.1 us (2%)
    psum x8, blocking collectives, shards(): zmean = lax.psum(jnp.sum(cap_var, axis=1), 'hour') / hours_all  281 us
    psum x8, waiting for transfers between devices, shards(): image = lax.psum(partial_rows, 'reg')  50.4 us
    dot_general x8, matrix products, shards(): jnp.einsum('shr,rc->shc', dual_low, matrix, preferred_element_type=jnp.fl...  30 us
    ppermute x8, starting transfers between devices, with_halo(): lax.ppermute(tail, axis, [(i, (i + 1) % count) for i in range(ends)])  23.9 us
    unnamed x65, local copies, waits for them, and re-layouts  10.4 us
    ppermute x8, starting transfers between devices, with_halo(): lax.ppermute(head, axis, [((i + 1) % count, i) for i in range(ends)])  10.3 us
    dot_general x8, matrix products, shards(): jnp.einsum('shc,rc->shr', primal_ext.astype(jnp.bfloat16), matrix, prefer...  10.2 us
    psum x1, blocking collectives, shards(): sum_total, mass_total = lax.psum((node_sum, node_mass), 'scen')  9.39 us
  transfers between devices with their start and end apart: 24, of which 8 were waited for; matrix products, arithmetic and copies ran while one was open for 3% of the time, Pallas kernels for 0%

commit v1 on v0

v1 whole, which is shorter than its diff:
```python
import jax
import jax.numpy as jnp
from jax import lax
from jax.experimental import pallas as pl
from jax.experimental.pallas import tpu as pltpu
from jax.sharding import PartitionSpec as P

ITERS = 8
RAMP_WEIGHT = 0.5
PENALTY = 1.0
STEP_PRIMAL = 0.3
STEP_INVEST = 0.5
STEP_DUAL = 0.3
STEP_CAP = 0.05

MESH = pl.DeviceIdType.MESH
HOURS_LOCAL = 168
HALVES = ((0, 80), (80, 88))
NH = 16
COLS_CORE = 512
COLS = 1024
CONS = 256
PAD = 8
F32 = jnp.float32
BF16 = jnp.bfloat16


def hop_order():
    def hops(d):
        y, z = d % 4, d // 4
        return min(y, 4 - y) + min(z, 4 - z)

    return sorted(range(1, NH), key=lambda d: -hops(d))


def kernel(
    cost_h, icost_h, tile_h, mask_h, dem_h, disp_h, dual_h, cap_h, inv_h, mult_h, cons_h, weight_s, node_s,
    disp_o, dual_o, inv_o, mult_o,
    cost_v, prim_v, a_v, capl_v, tile_v, mask_v, ml_v, m_v, mt_v, pre_v, dem_v,
    xs_v, xr_v, pr_v, p0s_v, p0r_v, he_v, hr_v, edge_v, h0s_v, h0r_v,
    il_v, ic_v, fold_v, frecv_v, invs_v, base_v, sb_v, wn_v, wnr_v, co_v, g_v, tmp_v, do_v,
    load_sem, xsend, xrecv, psend, precv, p0send, p0recv, hsend, hrecv, h0send, h0recv,
    csend, crecv, gsend, grecv, osend, orecv, oload,
):
    s_at, h_at, r_at = lax.axis_index("scen"), lax.axis_index("hour"), lax.axis_index("reg")
    core = lax.rem(r_at, 2)
    other = 1 - core
    r_core = r_at + 1 - 2 * core
    r_chip = lax.rem(r_at + 2, 4)
    y_at, z_at = lax.rem(h_at, 4), lax.div(h_at, 4)

    def hour_rel(d):
        return lax.rem(z_at + d // 4, 4) * 4 + lax.rem(y_at + d % 4, 4)

    order = hop_order()
    left, right = lax.rem(h_at + NH - 1, NH), lax.rem(h_at + 1, NH)
    peer_core = (s_at, h_at, r_core)
    peer_chip = (s_at, h_at, r_chip)
    peer_o0 = (1 - s_at, h_at, r_at)
    peer_o1 = (1 - s_at, h_at, r_core)

    greeted = [(s_at, hour_rel(d), r) for d in order for r in (r_at, r_core)]
    greeted += [peer_core, peer_chip, peer_o0, peer_o1]
    barrier = pltpu.get_barrier_semaphore()
    for peer in greeted:
        pl.semaphore_signal(barrier, inc=1, device_id=peer, device_id_type=MESH)

    own_pair = pl.ds(2 * core, 2)
    oth_pair = pl.ds(2 * other, 2)
    own_cols = pl.ds(pl.multiple_of(core * COLS_CORE, COLS_CORE), COLS_CORE)
    body_rows = pl.ds(PAD, HOURS_LOCAL)

    def load(n, src, dst):
        cp = pltpu.make_async_copy(src, dst, load_sem.at[n])
        cp.start()
        return cp

    c_cap = load(0, cap_h, capl_v)
    c_edge0 = load(1, disp_h.at[:, pl.ds(0, 8), :], edge_v.at[0])
    c_edge1 = load(2, disp_h.at[:, pl.ds(HOURS_LOCAL - 8, 8), :], edge_v.at[1])
    c_tile = load(3, tile_h.at[0], tile_v)
    c_mask = load(4, mask_h.at[0], mask_v)
    c_inv = load(5, inv_h, il_v.at[0])
    c_mult = load(6, mult_h, il_v.at[1])
    c_cons = load(7, cons_h, il_v.at[2])
    c_ic = load(8, icost_h, ic_v)
    c_disp = load(9, disp_h.at[own_pair], prim_v.at[0, :, body_rows, own_cols])
    c_a = load(10, cap_h.at[own_pair], a_v.at[:, :, own_cols])
    c_cost = load(11, cost_h.at[own_pair], cost_v.at[:, :, own_cols])
    c_dual = load(12, dual_h.at[own_pair], pre_v)
    c_dem = load(13, dem_h.at[own_pair], dem_v)

    c_cap.wait()
    for pair in range(2):
        for s in range(2):
            for i in range(4):
                p0s_v[pair, s, i:i + 1, :] = jnp.sum(
                    capl_v[2 * pair + s, :, 128 * i:128 * (i + 1)], axis=0, keepdims=True
                )
    p0r_v[core, h_at] = p0s_v[core]

    c_edge0.wait()
    c_edge1.wait()
    for s in range(4):
        h0s_v[0, s] = edge_v[0, s, 0:1, :]
        h0s_v[1, s] = edge_v[1, s, 7:8, :]

    c_tile.wait()
    c_mask.wait()
    ml_v[...] = tile_v[...] * mask_v[...].astype(BF16)

    c_inv.wait()
    c_mult.wait()
    c_cons.wait()
    c_ic.wait()
    for pair in range(2):
        for s in range(2):
            at = 2 * pair + s
            base = ic_v[...] + il_v[1, at] - PENALTY * il_v[2, at]
            cap0 = il_v[0, at]
            for g in range(3):
                for i in range(4):
                    lanes = slice(128 * i, 128 * (i + 1))
                    fold_v[pair, 0, s, g, i:i + 1, :] = cap0[g:g + 1, lanes]
                    fold_v[pair, 1, s, g, i:i + 1, :] = base[g:g + 1, lanes]

    for s in range(4):
        for g in range(3):
            wn_v[4 * s + g:4 * s + g + 1, :] = jnp.full((1, 128), node_s[g, s].astype(F32), F32)
        wn_v[4 * s + 3:4 * s + 4, :] = jnp.full((1, 128), weight_s[s], F32)

    pl.semaphore_wait(barrier, len(greeted))

    def send(src, dst, ssem, rsem, peer):
        cp = pltpu.make_async_remote_copy(
            src_ref=src, dst_ref=dst, send_sem=ssem, recv_sem=rsem, device_id=peer, device_id_type=MESH
        )
        cp.start()
        return cp

    first = []
    for d in order + [0]:
        for cross in (0, 1):
            if d == 0 and cross == 0:
                continue
            peer = (s_at, hour_rel(d), r_core if cross else r_at)
            first.append(send(
                p0s_v.at[other if cross else core], p0r_v.at[core, h_at],
                p0send.at[cross, d], p0recv.at[cross, d], peer,
            ))
    start_halo = []
    for side, to in ((0, left), (1, right)):
        for cross in (0, 1):
            peer = (s_at, to, r_core if cross else r_at)
            pair = oth_pair if cross else own_pair
            start_halo.append(send(
                h0s_v.at[side, pair], h0r_v.at[1 - side, core],
                h0send.at[side, cross], h0recv.at[side, cross], peer,
            ))
    swaps = [
        send(ml_v, m_v.at[:, own_cols], csend.at[0], crecv.at[0], peer_core),
        send(fold_v.at[other], frecv_v, csend.at[1], crecv.at[1], peer_core),
        send(disp_h.at[oth_pair], prim_v.at[0, :, body_rows, own_cols], csend.at[2], crecv.at[2], peer_core),
        send(cap_h.at[oth_pair], a_v.at[:, :, own_cols], csend.at[3], crecv.at[3], peer_core),
        send(cost_h.at[oth_pair], cost_v.at[:, :, own_cols], csend.at[4], crecv.at[4], peer_core),
    ]
    weights = send(wn_v, wnr_v, csend.at[5], crecv.at[5], peer_o0)
    c_ml = load(14, ml_v, m_v.at[:, own_cols])

    c_ml.wait()
    swaps[0].wait()
    for j in range(4):
        mt_v[256 * j:256 * (j + 1), :] = m_v[:, 256 * j:256 * (j + 1)].T
    swaps[1].wait()
    for s in range(2):
        for g in range(3):
            for n, dest in ((0, invs_v), (1, base_v)):
                mine, its = fold_v[core, n, s, g], frecv_v[n, s, g]
                dest[s, g] = jnp.concatenate(
                    [jnp.where(core == 0, mine, its), jnp.where(core == 0, its, mine)], axis=0
                )
    sb_v[...] = jnp.zeros_like(sb_v)
    weights.wait()

    def row_of(s, g):
        ref = wn_v if s < 4 else wnr_v
        at = 4 * (s % 4) + g
        return ref[at:at + 1, :]

    for g in range(3):
        nodes = [row_of(s, g) for s in range(8)]
        for s in range(4):
            parts = [jnp.where(nodes[t] == nodes[s], row_of(t, 3), 0.0) for t in range(8)]
            mass = ((parts[0] + parts[1]) + (parts[2] + parts[3])) + ((parts[4] + parts[5]) + (parts[6] + parts[7]))
            scale = 1.0 / (mass + jnp.where(mass <= 0.0, 1.0, 0.0))
            for t in range(8):
                at = (3 * s + g) * 8 + t
                co_v[at:at + 1, :] = parts[t] * scale

    for cp in start_halo:
        cp.wait()
    c_disp.wait()
    swaps[2].wait()
    keep_left = jnp.where(h_at > 0, 1.0, 0.0).astype(F32)
    keep_right = jnp.where(h_at < NH - 1, 1.0, 0.0).astype(F32)
    for s in range(2):
        for src in range(2):
            lanes = slice(COLS_CORE * src, COLS_CORE * (src + 1))
            prim_v[0, s, PAD - 1:PAD, lanes] = h0r_v[0, src, s] * keep_left
            prim_v[0, s, PAD + HOURS_LOCAL:PAD + HOURS_LOCAL + 1, lanes] = h0r_v[1, src, s] * keep_right
    c_a.wait()
    swaps[3].wait()
    c_cost.wait()
    swaps[4].wait()
    c_dual.wait()
    c_dem.wait()

    def image_copy(slot, s, half):
        rows = pl.ds(2 * HALVES[half][0], 2 * HALVES[half][1])
        return pltpu.make_async_remote_copy(
            src_ref=xs_v.at[s, rows], dst_ref=xr_v.at[slot, s, rows],
            send_sem=xsend.at[s, half], recv_sem=xrecv.at[slot, s, half],
            device_id=peer_chip, device_id_type=MESH,
        )

    def halo_copy(slot, side, s):
        return pltpu.make_async_remote_copy(
            src_ref=he_v.at[side, s], dst_ref=hr_v.at[slot, 1 - side, s],
            send_sem=hsend.at[side, s], recv_sem=hrecv.at[slot, 1 - side, s],
            device_id=(s_at, left if side == 0 else right, r_at), device_id_type=MESH,
        )

    def sum_copy(slot, d):
        return pltpu.make_async_remote_copy(
            src_ref=pr_v.at[slot, h_at], dst_ref=pr_v.at[slot, h_at],
            send_sem=psend.at[slot, d], recv_sem=precv.at[slot, d],
            device_id=(s_at, hour_rel(d), r_at), device_id_type=MESH,
        )

    def dual_update(last, s, half):
        r0, n = HALVES[half]
        rows = pl.ds(r0, n)
        image_copy(last, s, half).wait_recv()
        got = xr_v[last, s, 2 * r0:2 * (r0 + n), :].astype(F32)
        got = jnp.concatenate([got[:n], got[n:]], axis=1)
        pre_v[s, rows, :] = jnp.maximum(pre_v[s, rows, :] - STEP_DUAL * got, 0.0)

    def chunk(k, now, s, half):
        r0, n = HALVES[half]
        nxt = 1 - now

        @pl.when(k > 0)
        def _():
            dual_update(nxt, s, half)
            side = half
            halo_copy(now, 1 - side, s).wait_recv()
            if half == 0:
                prim_v[now, s, PAD - 1:PAD, :] = hr_v[now, 0, s] * keep_left
            else:
                prim_v[now, s, PAD + HOURS_LOCAL:PAD + HOURS_LOCAL + 1, :] = hr_v[now, 1, s] * keep_right

        dual = pre_v[s, r0:r0 + n, :]
        low = dual.astype(BF16)
        image = None
        for j in range(4):
            cols = slice(256 * j, 256 * (j + 1))
            pulled = jnp.dot(low, m_v[:, cols], preferred_element_type=F32)
            p = prim_v[now, s, PAD + r0:PAD + r0 + n, cols]
            up = prim_v[now, s, PAD + r0 - 1:PAD + r0 + n - 1, cols]
            down = prim_v[now, s, PAD + r0 + 1:PAD + r0 + n + 1, cols]
            sb = jnp.concatenate([sb_v[s, 2 * j:2 * j + 1, :], sb_v[s, 2 * j + 1:2 * j + 2, :]], axis=1)
            cap = jnp.maximum(a_v[s, r0:r0 + n, cols] - sb, 0.0)
            rest = (cost_v[s, r0:r0 + n, cols] - pulled) + cap
            fresh = (
                (1.0 - 2.0 * RAMP_WEIGHT * STEP_PRIMAL) * p
                + (RAMP_WEIGHT * STEP_PRIMAL) * (up + down)
                - STEP_PRIMAL * rest
            )
            fresh = jnp.maximum(fresh, 0.0)
            ext = 2.0 * fresh - p
            prim_v[nxt, s, PAD + r0:PAD + r0 + n, cols] = fresh
            a_v[s, r0:r0 + n, cols] = cap + STEP_CAP * ext
            part = jnp.dot(ext.astype(BF16), mt_v[cols, :], preferred_element_type=F32)
            image = part if image is None else image + part

        @pl.when(k > 0)
        def _():
            image_copy(now, s, half).wait_send()

        xs_v[s, 2 * r0:2 * (r0 + n), :] = jnp.concatenate([image[:, :128], image[:, 128:]], axis=0).astype(BF16)
        image_copy(now, s, half).start()
        pre_v[s, r0:r0 + n, :] = dual + STEP_DUAL * (dem_v[s, r0:r0 + n, :] - image)

        @pl.when(k < ITERS - 1)
        def _():
            side = half

            @pl.when(k > 0)
            def _():
                halo_copy(nxt, side, s).wait_send()

            row = PAD if half == 0 else PAD + HOURS_LOCAL - 1
            he_v[side, s] = prim_v[nxt, s, row:row + 1, :]
            halo_copy(nxt, side, s).start()

    def invest_step(total, s):
        mean = total * (1.0 / (NH * HOURS_LOCAL))
        spent = None
        for g in range(3):
            inv = invs_v[s, g]
            grad = base_v[s, g] + PENALTY * inv - mean
            new = jnp.maximum(inv - STEP_INVEST * grad, 0.0)
            invs_v[s, g] = new
            ext = 2.0 * new - inv
            spent = ext if spent is None else spent + ext
        sb_v[s] = STEP_CAP * spent

    def sums_in(k, now):
        @pl.when(k == 0)
        def _():
            for cp in first:
                cp.wait()
            for s in range(2):
                parts = []
                for src in range(2):
                    total = p0r_v[src, 0, s]
                    for h in range(1, NH):
                        total = total + p0r_v[src, h, s]
                    parts.append(total)
                invest_step(jnp.concatenate(parts, axis=0), s)

        @pl.when(k > 0)
        def _():
            for d in order:
                sum_copy(now, d).wait_send()
            for d in order[::-1]:
                sum_copy(now, d).wait_recv()
            for s in range(2):
                parts = [pr_v[now, h, s] for h in range(NH)]
                while len(parts) > 1:
                    parts = [parts[i] + parts[i + 1] for i in range(0, len(parts), 2)]
                invest_step(parts[0], s)

    def step(k, carry):
        now = lax.rem(k, 2)
        nxt = 1 - now
        for s in range(2):
            for half in range(2):
                chunk(k, now, s, half)
        sums_in(k, now)

        @pl.when(k < ITERS - 1)
        def _():
            for s in range(2):
                for j in range(8):
                    left_over = jnp.maximum(a_v[s, :, 128 * j:128 * (j + 1)] - sb_v[s, j:j + 1, :], 0.0)
                    pr_v[nxt, h_at, s, j:j + 1, :] = jnp.sum(left_over, axis=0, keepdims=True)
            for d in order:
                sum_copy(nxt, d).start()

        @pl.when(k == ITERS - 1)
        def _():
            g_v[0, core] = invs_v[...]

        return carry

    lax.fori_loop(0, ITERS, step, 0)

    gathers = [
        send(g_v.at[0, core], g_v.at[1, core], gsend.at[1], grecv.at[1], peer_o0),
        send(g_v.at[0, core], g_v.at[1, core], gsend.at[2], grecv.at[2], peer_o1),
        send(g_v.at[0, core], g_v.at[0, core], gsend.at[0], grecv.at[0], peer_core),
    ]
    end = ITERS % 2
    outs = [
        send(
            prim_v.at[end, :, body_rows, pl.ds(pl.multiple_of(other * COLS_CORE, COLS_CORE), COLS_CORE)],
            disp_o.at[own_pair], osend.at[0], orecv.at[0], peer_core,
        )
    ]
    c_own = pltpu.make_async_copy(prim_v.at[end, :, body_rows, own_cols], disp_o.at[own_pair], oload.at[0])
    c_own.start()

    on_first = jnp.where(r_at < 2, 1.0, 0.0).astype(F32) > 0.5
    for s in range(2):
        for half in range(2):
            image_copy(1 - end, s, half).wait_send()
            dual_update(1 - end, s, half)
        d = pre_v[s]
        d = jnp.where(on_first, d[:, :128], d[:, 128:])
        lo, hi = d[:, :64], d[:, 64:]
        do_v[0, s] = jnp.where(core == 0, lo, hi)
        do_v[1, s] = jnp.where(core == 0, hi, lo)
    outs.append(send(do_v.at[1], dual_o.at[own_pair], osend.at[1], orecv.at[1], peer_core))
    c_dual_own = pltpu.make_async_copy(do_v.at[0], dual_o.at[own_pair], oload.at[1])
    c_dual_own.start()
    for side in range(2):
        for s in range(2):
            halo_copy(end, side, s).wait_send()

    for cp in gathers[::-1]:
        cp.wait()
    for g in range(3):
        invs = [g_v[t // 4, (t // 2) % 2, t % 2, g] for t in range(8)]
        for s in range(4):
            spread = None
            for t in range(8):
                at = (3 * s + g) * 8 + t
                term = co_v[at:at + 1, :] * invs[t]
                spread = term if spread is None else spread + term
            tmp_v[0, 3 * s + g] = invs[s]
            tmp_v[1, 3 * s + g] = PENALTY * (invs[s] - spread)
    for s in range(4):
        for g in range(3):
            for i in range(4):
                lanes = slice(128 * i, 128 * (i + 1))
                inv_o[s, g:g + 1, lanes] = tmp_v[0, 3 * s + g, pl.ds(4 * core + i, 1), :]
                mult_o[s, g:g + 1, lanes] = il_v[1, s, g:g + 1, lanes] + tmp_v[1, 3 * s + g, pl.ds(4 * core + i, 1), :]
    for cp in outs:
        cp.wait()
    c_own.wait()
    c_dual_own.wait()


def shards(*args):
    hbm = pl.BlockSpec(memory_space=pltpu.HBM)
    vmem = pl.BlockSpec(memory_space=pltpu.VMEM)
    smem = pl.BlockSpec(memory_space=pltpu.SMEM)
    dma = pltpu.SemaphoreType.DMA
    return pl.pallas_call(
        kernel,
        out_shape=(
            jax.ShapeDtypeStruct((4, HOURS_LOCAL, COLS_CORE), F32),
            jax.ShapeDtypeStruct((4, HOURS_LOCAL, 64), F32),
            jax.ShapeDtypeStruct((4, 3, COLS_CORE), F32),
            jax.ShapeDtypeStruct((4, 3, COLS_CORE), F32),
        ),
        in_specs=[hbm] * 11 + [smem] * 2,
        out_specs=(hbm, hbm, vmem, vmem),
        scratch_shapes=[
            pltpu.VMEM((2, HOURS_LOCAL, COLS), F32),
            pltpu.VMEM((2, 2, HOURS_LOCAL + 2 * PAD, COLS), F32),
            pltpu.VMEM((2, HOURS_LOCAL, COLS), F32),
            pltpu.VMEM((4, HOURS_LOCAL, COLS_CORE), F32),
            pltpu.VMEM((CONS, COLS_CORE), BF16),
            pltpu.VMEM((CONS, COLS_CORE), jnp.int32),
            pltpu.VMEM((CONS, COLS_CORE), BF16),
            pltpu.VMEM((CONS, COLS), BF16),
            pltpu.VMEM((COLS, CONS), BF16),
            pltpu.VMEM((2, HOURS_LOCAL, CONS), F32),
            pltpu.VMEM((2, HOURS_LOCAL, CONS), F32),
            pltpu.VMEM((2, 2 * HOURS_LOCAL, 128), BF16),
            pltpu.VMEM((2, 2, 2 * HOURS_LOCAL, 128), BF16),
            pltpu.VMEM((2, NH, 2, 8, 128), F32),
            pltpu.VMEM((2, 2, 4, 128), F32),
            pltpu.VMEM((2, NH, 2, 4, 128), F32),
            pltpu.VMEM((2, 2, 1, COLS), F32),
            pltpu.VMEM((2, 2, 2, 1, COLS), F32),
            pltpu.VMEM((2, 4, 8, COLS_CORE), F32),
            pltpu.VMEM((2, 4, 1, COLS_CORE), F32),
            pltpu.VMEM((2, 2, 2, 1, COLS_CORE), F32),
            pltpu.VMEM((3, 4, 3, COLS_CORE), F32),
            pltpu.VMEM((3, COLS_CORE), F32),
            pltpu.VMEM((2, 2, 2, 3, 4, 128), F32),
            pltpu.VMEM((2, 2, 3, 4, 128), F32),
            pltpu.VMEM((2, 3, 8, 128), F32),
            pltpu.VMEM((2, 3, 8, 128), F32),
            pltpu.VMEM((2, 8, 128), F32),
            pltpu.VMEM((16, 128), F32),
            pltpu.VMEM((16, 128), F32),
            pltpu.VMEM((96, 128), F32),
            pltpu.VMEM((2, 2, 2, 3, 8, 128), F32),
            pltpu.VMEM((2, 12, 8, 128), F32),
            pltpu.VMEM((2, 2, HOURS_LOCAL, 64), F32),
            dma((15,)),
            dma((2, 2)), dma((2, 2, 2)),
            dma((2, NH)), dma((2, NH)),
            dma((2, NH)), dma((2, NH)),
            dma((2, 2)), dma((2, 2, 2)),
            dma((2, 2)), dma((2, 2)),
            dma((6,)), dma((6,)),
            dma((3,)), dma((3,)),
            dma((2,)), dma((2,)), dma((2,)),
        ],
        compiler_params=pltpu.CompilerParams(
            collective_id=0, has_side_effects=True, vmem_limit_bytes=48 * 2**20
        ),
        cost_estimate=pl.CostEstimate(flops=3 * 10**9, bytes_accessed=9 * 10**6, transcendentals=0),
    )(*args)


def solution(mesh):
    placed = (
        P("scen", "hour", "reg"),
        P(None, "reg"),
        P("hour", None, "reg"),
        P("hour", None, "reg"),
        P("scen", "hour", None),
        P("scen", "hour", "reg"),
        P("scen", "hour", None),
        P("scen", "hour", "reg"),
        P("scen", None, "reg"),
        P("scen", None, "reg"),
        P("scen", None, "reg"),
        P("scen"),
        P(None, "scen"),
    )
    return jax.shard_map(
        shards,
        mesh=mesh,
        in_specs=placed,
        out_specs=(
            P("scen", "hour", "reg"),
            P("scen", "hour", "reg"),
            P("scen", None, "reg"),
            P("scen", None, "reg"),
        ),
        check_vma=False,
    )
```

time: 459 us -> 72.5 us (0.16)
  blocking collectives: 290 us -> 0 us
  Pallas kernels: 0 us -> 58.2 us
  waiting for transfers between devices: 50.6 us -> 0 us
  matrix products: 41.5 us -> 0 us
  starting transfers between devices: 34.5 us -> 0 us
  between operations: 14.8 us -> 0.66 us
  other arithmetic: 10.1 us -> 0 us
    psum x9 -> x0, blocking collectives: 290 us -> none  [the longest x8 281 us: shards(): zmean = lax.psum(jnp.sum(cap_var, axis=1), 'hour') / hours_all]
    pallas_call x0 -> x1, Pallas kernels: none -> 58.2 us  [shards(): pl.pallas_call(kernel, out_shape=(jax.ShapeDtypeStruct((4, HOURS_LOCAL, C...]
    psum x8 -> x0, waiting for transfers between devices: 50.4 us -> none  [shards(): image = lax.psum(partial_rows, 'reg')]
    dot_general x19 -> x0, matrix products: 41.5 us -> none  [the longest x8 30 us: shards(): jnp.einsum('shr,rc->shc', dual_low, matrix, preferred_element_type=jnp.fl...]
    ppermute x16 -> x0, starting transfers between devices: 34.2 us -> none  [the longest x8 23.9 us: with_halo(): lax.ppermute(tail, axis, [(i, (i + 1) % count) for i in range(ends)])]
    max x5 -> x0, other arithmetic: 6.96 us -> none  [the longest x4 6.85 us: shards(): dual_var = jnp.maximum(dual_var + STEP_DUAL * (demand - image), 0.0)]
    slice x8 -> x0, local copies, waits for them, and re-layouts: 6.39 us -> none  [with_halo(): lax.slice_in_dim(cells, cells.shape[dim] - width, cells.shape[dim], axis=...]
    unnamed x65 -> x20, local copies, waits for them, and re-layouts: 10.4 us -> 10.9 us
  transfers between devices with their start and end apart: 24 -> 0, of which waited for: 8 -> 0; matrix products, arithmetic and copies ran while one was open for 3% -> 0% of each run, Pallas kernels for 0% -> 0%
where the time goes in v1:
time: 72.5 us; the launch traced here: 71.9 us
  Pallas kernels  58.2 us (80%)
  local copies, waits for them, and re-layouts  13 us (18%)
    pallas_call x1, Pallas kernels, shards(): pl.pallas_call(kernel, out_shape=(jax.ShapeDtypeStruct((4, HOURS_LOCAL, C...  58.2 us
    unnamed x20, local copies, waits for them, and re-layouts  10.9 us
    pallas_call x3, local copies, waits for them, and re-layouts, shards(): pl.pallas_call(kernel, out_shape=(jax.ShapeDtypeStruct((4, HOURS_LOCAL, C...  2.12 us

profile of v1, /device:TPU:1, one launch (start us, length us, event | category | flops | bytes accessed | tf_op | source)
XLA Modules:
  0.0 71.9 jit_solution(6877248170430094961)
XLA Ops:
  0.6 0.8 %copy.17.inv_h = f32[4,3,512]{2,1,0:T(4,128)S(1)} copy(f32[4,3,512]{2,0,1:T(4,128)} %param.21) | data formatting | bytes 49152 | tf_op args[8]
  1.4 0.8 %copy.18.mult_h = f32[4,3,512]{2,1,0:T(4,128)S(1)} copy(f32[4,3,512]{2,0,1:T(4,128)} %param.22) | data formatting | bytes 49152 | tf_op args[9]
  2.1 0.8 %copy.19.cons_h = f32[4,3,512]{2,1,0:T(4,128)S(1)} copy(f32[4,3,512]{2,0,1:T(4,128)} %param.23) | data formatting | bytes 49152 | tf_op args[10]
  2.9 0.0 copy-start
  2.9 1.3 %copy-done = f32[4,168,512]{2,1,0:T(8,128)S(1)} copy-done((f32[4,168,512]{2,1,0:T(8,128)S(1)}, f32[4,168,512]{2,1,0:T(8,128)}, u32[]{:S(2)}) %copy-start) | copy-done | bytes 1376280
  4.2 0.0 copy-start.1
  4.2 1.1 %copy-done.1 = f32[4,168,256]{2,1,0:T(8,128)S(1)} copy-done((f32[4,168,256]{2,1,0:T(8,128)S(1)}, f32[4,168,256]{2,1,0:T(8,128)}, u32[]{:S(2)}) %copy-start.1) | copy-done | bytes 688152
  5.3 0.0 copy-start.2
  5.3 1.1 %copy-done.2 = f32[4,168,256]{2,1,0:T(8,128)S(1)} copy-done((f32[4,168,256]{2,1,0:T(8,128)S(1)}, f32[4,168,256]{2,1,0:T(8,128)}, u32[]{:S(2)}) %copy-start.2) | copy-done | bytes 688152
  6.4 0.0 copy-start.3
  6.4 1.0 %copy-done.3 = s32[1,256,512]{2,1,0:T(8,128)S(1)} copy-done((s32[1,256,512]{2,1,0:T(8,128)S(1)}, s32[1,256,512]{2,1,0:T(8,128)}, u32[]{:S(2)}) %copy-start.3) | copy-done | bytes 524312
  7.5 0.0 copy-start.4
  7.5 0.9 %copy-done.4 = bf16[1,256,512]{2,1,0:T(8,128)(2,1)S(1)} copy-done((bf16[1,256,512]{2,1,0:T(8,128)(2,1)S(1)}, bf16[1,256,512]{2,1,0:T(8,128)(2,1)}, u32[]{:S(2)}) %copy-start.4) | copy-done | bytes 262168
  8.4 0.0 copy-start.5
  8.4 0.7 copy-done.5
  9.1 0.0 copy-start.6
  9.1 0.7 copy-done.6
  9.8 0.0 copy-start.7
  9.8 0.7 copy-done.7
  10.5 58.2 %shard_map.156 = (f32[4,168,512]{2,1,0:T(8,128)S(1)}, f32[4,168,64]{2,1,0:T(8,128)S(1)}, f32[4,3,512]{2,1,0:T(4,128)S(1)}, f32[4,3,512]{2,1,0:T(4,128)S(1)}) custom-call(f32[4,168,512]{2,1,0:T(8,128)S(1)} %copy-done, f32[3,512]{1,0:T(4,128)S(1)} %copy-done.5, bf16[1,256,512]{2,1,0:T(8,128)(2,1)S(1)} %copy-done.4, s32[1,256,512]{2,1,0:T(8,128)S(1)} %copy-done.3, ...), custom_call_target="tpu_custom_call" | custom-call | flops 3000000000 | bytes 9000000 | tf_op jit(solution)/shard_map/pallas_call | solution.py:430
  68.7 0.6 copy.21
  69.3 0.6 copy.22
  70.0 0.9 %copy.20 = f32[4,168,64]{1,2,0:T(8,128)} copy(f32[4,168,64]{2,1,0:T(8,128)S(1)} %get-tuple-element.5) | data formatting | bytes 344064 | tf_op jit(solution)/shard_map/pallas_call | solution.py:430
  70.8 1.1 %copy.24 = f32[4,168,512]{2,1,0:T(8,128)} copy(f32[4,168,512]{2,1,0:T(8,128)S(1)} %get-tuple-element.12) | data formatting | bytes 2752512
Async XLA Ops:
  2.9 1.3 %copy-start = (f32[4,168,512]{2,1,0:T(8,128)S(1)}, f32[4,168,512]{2,1,0:T(8,128)}, u32[]{:S(2)}) copy-start(f32[4,168,512]{2,1,0:T(8,128)} %cost_h.1) | copy-start | bytes 4128772
  4.2 1.1 %copy-start.1 = (f32[4,168,256]{2,1,0:T(8,128)S(1)}, f32[4,168,256]{2,1,0:T(8,128)}, u32[]{:S(2)}) copy-start(f32[4,168,256]{2,1,0:T(8,128)} %dem_h.1) | copy-start | bytes 2064388
  5.3 1.1 %copy-start.2 = (f32[4,168,256]{2,1,0:T(8,128)S(1)}, f32[4,168,256]{2,1,0:T(8,128)}, u32[]{:S(2)}) copy-start(f32[4,168,256]{2,1,0:T(8,128)} %dual_h.1) | copy-start | bytes 2064388
  6.4 1.0 %copy-start.3 = (s32[1,256,512]{2,1,0:T(8,128)S(1)}, s32[1,256,512]{2,1,0:T(8,128)}, u32[]{:S(2)}) copy-start(s32[1,256,512]{2,1,0:T(8,128)} %mask_h.1) | copy-start | bytes 1572868
  7.5 0.9 %copy-start.4 = (bf16[1,256,512]{2,1,0:T(8,128)(2,1)S(1)}, bf16[1,256,512]{2,1,0:T(8,128)(2,1)}, u32[]{:S(2)}) copy-start(bf16[1,256,512]{2,1,0:T(8,128)(2,1)} %tile_h.1) | copy-start | bytes 786436
  8.4 0.7 copy-start.5
  9.1 0.7 copy-start.6
  9.8 0.7 copy-start.7

commit v2 on v1

--- a/solution.py
+++ b/solution.py
@@ -34,11 +34,11 @@
 
 
 def kernel(
-    cost_h, icost_h, tile_h, mask_h, dem_h, disp_h, dual_h, cap_h, inv_h, mult_h, cons_h, weight_s, node_s,
+    cost_h, icost_h, tile_h, mask_h, dem_h, disp_h, dual_h, cap_h, inv_h, mult_h, cons_h, weight_h, node_h,
     disp_o, dual_o, inv_o, mult_o,
     cost_v, prim_v, a_v, capl_v, tile_v, mask_v, ml_v, m_v, mt_v, pre_v, dem_v,
     xs_v, xr_v, pr_v, p0s_v, p0r_v, he_v, hr_v, edge_v, h0s_v, h0r_v,
-    il_v, ic_v, fold_v, frecv_v, invs_v, base_v, sb_v, wn_v, wnr_v, co_v, g_v, tmp_v, do_v,
+    il_v, ic_v, fold_v, frecv_v, invs_v, base_v, sb_v, wn_v, wnr_v, co_v, g_v, tmp_v, do_v, weight_s, node_s,
     load_sem, xsend, xrecv, psend, precv, p0send, p0recv, hsend, hrecv, h0send, h0recv,
     csend, crecv, gsend, grecv, osend, orecv, oload,
 ):
@@ -84,6 +84,8 @@
     c_mult = load(6, mult_h, il_v.at[1])
     c_cons = load(7, cons_h, il_v.at[2])
     c_ic = load(8, icost_h, ic_v)
+    c_weight = load(15, weight_h, weight_s)
+    c_node = load(16, node_h, node_s)
     c_disp = load(9, disp_h.at[own_pair], prim_v.at[0, :, body_rows, own_cols])
     c_a = load(10, cap_h.at[own_pair], a_v.at[:, :, own_cols])
     c_cost = load(11, cost_h.at[own_pair], cost_v.at[:, :, own_cols])
@@ -116,14 +118,16 @@
     for pair in range(2):
         for s in range(2):
             at = 2 * pair + s
-            base = ic_v[...] + il_v[1, at] - PENALTY * il_v[2, at]
-            cap0 = il_v[0, at]
             for g in range(3):
+                cap0 = il_v[0, g, at:at + 1, :]
+                base = ic_v[g:g + 1, :] + il_v[1, g, at:at + 1, :] - PENALTY * il_v[2, g, at:at + 1, :]
                 for i in range(4):
                     lanes = slice(128 * i, 128 * (i + 1))
-                    fold_v[pair, 0, s, g, i:i + 1, :] = cap0[g:g + 1, lanes]
-                    fold_v[pair, 1, s, g, i:i + 1, :] = base[g:g + 1, lanes]
-
+                    fold_v[pair, 0, s, g, i:i + 1, :] = cap0[:, lanes]
+                    fold_v[pair, 1, s, g, i:i + 1, :] = base[:, lanes]
+
+    c_weight.wait()
+    c_node.wait()
     for s in range(4):
         for g in range(3):
             wn_v[4 * s + g:4 * s + g + 1, :] = jnp.full((1, 128), node_s[g, s].astype(F32), F32)
@@ -387,8 +391,8 @@
             image_copy(1 - end, s, half).wait_send()
             dual_update(1 - end, s, half)
         d = pre_v[s]
-        d = jnp.where(on_first, d[:, :128], d[:, 128:])
-        lo, hi = d[:, :64], d[:, 64:]
+        d = jnp.where(on_first, d[:, :128], d[:, 128:]).T
+        lo, hi = d[:64], d[64:]
         do_v[0, s] = jnp.where(core == 0, lo, hi)
         do_v[1, s] = jnp.where(core == 0, hi, lo)
     outs.append(send(do_v.at[1], dual_o.at[own_pair], osend.at[1], orecv.at[1], peer_core))
@@ -414,8 +418,8 @@
         for g in range(3):
             for i in range(4):
                 lanes = slice(128 * i, 128 * (i + 1))
-                inv_o[s, g:g + 1, lanes] = tmp_v[0, 3 * s + g, pl.ds(4 * core + i, 1), :]
-                mult_o[s, g:g + 1, lanes] = il_v[1, s, g:g + 1, lanes] + tmp_v[1, 3 * s + g, pl.ds(4 * core + i, 1), :]
+                inv_o[g, s:s + 1, lanes] = tmp_v[0, 3 * s + g, pl.ds(4 * core + i, 1), :]
+                mult_o[g, s:s + 1, lanes] = il_v[1, g, s:s + 1, lanes] + tmp_v[1, 3 * s + g, pl.ds(4 * core + i, 1), :]
     for cp in outs:
         cp.wait()
     c_own.wait()
@@ -423,19 +427,19 @@
 
 
 def shards(*args):
+    args = args[:8] + tuple(jnp.transpose(x, (1, 0, 2)) for x in args[8:11]) + args[11:]
     hbm = pl.BlockSpec(memory_space=pltpu.HBM)
     vmem = pl.BlockSpec(memory_space=pltpu.VMEM)
-    smem = pl.BlockSpec(memory_space=pltpu.SMEM)
     dma = pltpu.SemaphoreType.DMA
-    return pl.pallas_call(
+    disp, dual, inv, mult = pl.pallas_call(
         kernel,
         out_shape=(
             jax.ShapeDtypeStruct((4, HOURS_LOCAL, COLS_CORE), F32),
-            jax.ShapeDtypeStruct((4, HOURS_LOCAL, 64), F32),
-            jax.ShapeDtypeStruct((4, 3, COLS_CORE), F32),
-            jax.ShapeDtypeStruct((4, 3, COLS_CORE), F32),
+            jax.ShapeDtypeStruct((4, 64, HOURS_LOCAL), F32),
+            jax.ShapeDtypeStruct((3, 4, COLS_CORE), F32),
+            jax.ShapeDtypeStruct((3, 4, COLS_CORE), F32),
         ),
-        in_specs=[hbm] * 11 + [smem] * 2,
+        in_specs=[hbm] * 13,
         out_specs=(hbm, hbm, vmem, vmem),
         scratch_shapes=[
             pltpu.VMEM((2, HOURS_LOCAL, COLS), F32),
@@ -459,7 +463,7 @@
             pltpu.VMEM((2, 4, 8, COLS_CORE), F32),
             pltpu.VMEM((2, 4, 1, COLS_CORE), F32),
             pltpu.VMEM((2, 2, 2, 1, COLS_CORE), F32),
-            pltpu.VMEM((3, 4, 3, COLS_CORE), F32),
+            pltpu.VMEM((3, 3, 4, COLS_CORE), F32),
             pltpu.VMEM((3, COLS_CORE), F32),
             pltpu.VMEM((2, 2, 2, 3, 4, 128), F32),
             pltpu.VMEM((2, 2, 3, 4, 128), F32),
@@ -471,8 +475,10 @@
             pltpu.VMEM((96, 128), F32),
             pltpu.VMEM((2, 2, 2, 3, 8, 128), F32),
             pltpu.VMEM((2, 12, 8, 128), F32),
-            pltpu.VMEM((2, 2, HOURS_LOCAL, 64), F32),
-            dma((15,)),
+            pltpu.VMEM((2, 2, 64, HOURS_LOCAL), F32),
+            pltpu.SMEM((4,), F32),
+            pltpu.SMEM((3, 4), jnp.int32),
+            dma((17,)),
             dma((2, 2)), dma((2, 2, 2)),
             dma((2, NH)), dma((2, NH)),
             dma((2, NH)), dma((2, NH)),
@@ -483,10 +489,11 @@
             dma((2,)), dma((2,)), dma((2,)),
         ],
         compiler_params=pltpu.CompilerParams(
-            collective_id=0, has_side_effects=True, vmem_limit_bytes=48 * 2**20
+            collective_id=0, has_side_effects=True, vmem_limit_bytes=58 * 2**20
         ),
         cost_estimate=pl.CostEstimate(flops=3 * 10**9, bytes_accessed=9 * 10**6, transcendentals=0),
     )(*args)
+    return disp, jnp.transpose(dual, (0, 2, 1)), jnp.transpose(inv, (1, 0, 2)), jnp.transpose(mult, (1, 0, 2))
 
 
 def solution(mesh):

time: 72.5 us -> 63.6 us (0.88)
  local copies, waits for them, and re-layouts: 13 us -> 4.49 us
    unnamed x20 -> x10, local copies, waits for them, and re-layouts: 10.9 us -> 4.49 us
    pallas_call x3 -> x0, local copies, waits for them, and re-layouts: 2.12 us -> none  [shards(): pl.pallas_call(kernel, out_shape=(jax.ShapeDtypeStruct((4, HOURS_LOCAL, C...]
where the time goes in v2:
time: 63.6 us; the launch traced here: 63.5 us
  Pallas kernels  58.3 us (92%)
  local copies, waits for them, and re-layouts  4.49 us (7%)
  between operations  0.67 us (1%)
    pallas_call x1, Pallas kernels, shards(): pl.pallas_call(kernel, out_shape=(jax.ShapeDtypeStruct((4, HOURS_LOCAL, C...  58.3 us
    unnamed x10, local copies, waits for them, and re-layouts  4.49 us

profile of v2, /device:TPU:1, one launch (start us, length us, event | category | flops | bytes accessed | tf_op | source)
XLA Modules:
  0.0 63.5 jit_solution(18020367055057159793)
XLA Ops:
  0.6 58.3 %shard_map.156 = (f32[4,168,512]{2,1,0:T(8,128)}, f32[4,64,168]{2,1,0:T(8,128)}, f32[3,4,512]{2,1,0:T(4,128)}, f32[3,4,512]{2,1,0:T(4,128)}) custom-call(f32[4,168,512]{2,1,0:T(8,128)} %cost_h.1, f32[3,512]{1,0:T(4,128)} %icost_h.1, bf16[1,256,512]{2,1,0:T(8,128)(2,1)} %tile_h.1, s32[1,256,512]{2,1,0:T(8,128)} %mask_h.1, f32[4,168,256]{2,1,0:T(8,128)} %dem_h.1, ...), custom_call_target="tpu_custom_call" | custom-call | flops 3000000000 | bytes 9000000 | tf_op jit(solution)/shard_map/pallas_call | solution.py:434
  59.0 0.0 copy-start
  59.0 0.0 copy-start.2
  59.0 0.0 copy-start.1
  59.0 2.6 %copy.21 = f32[4,168,512]{2,1,0:T(8,128)} copy(f32[4,168,512]{2,1,0:T(8,128)} %get-tuple-element.16) | data formatting | bytes 2752512
  61.5 0.0 copy-done
  61.5 0.7 %copy.22 = f32[4,168,64]{1,2,0:T(8,128)} copy(f32[4,168,64]{1,2,0:T(8,128)S(1)} %bitcast.6) | data formatting | bytes 344064
  62.2 0.0 copy-done.2
  62.3 0.6 copy.23
  62.9 0.0 copy-done.1
  62.9 0.6 copy.24
Async XLA Ops:
  59.0 2.6 %copy-start = (f32[4,64,168]{2,1,0:T(8,128)S(1)}, f32[4,64,168]{2,1,0:T(8,128)}, u32[]{:S(2)}) copy-start(f32[4,64,168]{2,1,0:T(8,128)} %get-tuple-element.9) | copy-start | bytes 516100
  59.0 3.3 %copy-start.2 = (f32[3,4,512]{2,1,0:T(4,128)S(1)}, f32[3,4,512]{2,1,0:T(4,128)}, u32[]{:S(2)}) copy-start(f32[3,4,512]{2,1,0:T(4,128)} %get-tuple-element.10) | copy-start | bytes 73732
  59.0 3.9 %copy-start.1 = (f32[3,4,512]{2,1,0:T(4,128)S(1)}, f32[3,4,512]{2,1,0:T(4,128)}, u32[]{:S(2)}) copy-start(f32[3,4,512]{2,1,0:T(4,128)} %get-tuple-element.11) | copy-start | bytes 73732

commit v3 on v2

--- a/solution.py
+++ b/solution.py
@@ -15,7 +15,8 @@
 
 MESH = pl.DeviceIdType.MESH
 HOURS_LOCAL = 168
-HALVES = ((0, 80), (80, 88))
+PARTS = (((0, 40), (128, 40)), ((40, 88),))
+SENT = ((0, 160), (160, 176))
 NH = 16
 COLS_CORE = 512
 COLS = 1024
@@ -38,7 +39,7 @@
     disp_o, dual_o, inv_o, mult_o,
     cost_v, prim_v, a_v, capl_v, tile_v, mask_v, ml_v, m_v, mt_v, pre_v, dem_v,
     xs_v, xr_v, pr_v, p0s_v, p0r_v, he_v, hr_v, edge_v, h0s_v, h0r_v,
-    il_v, ic_v, fold_v, frecv_v, invs_v, base_v, sb_v, wn_v, wnr_v, co_v, g_v, tmp_v, do_v, weight_s, node_s,
+    il_v, ic_v, fold_v, frecv_v, invs_v, base_v, sb_v, wn_v, wnr_v, co_v, g_v, tmp_v, do_v, sum_v, weight_s, node_s,
     load_sem, xsend, xrecv, psend, precv, p0send, p0recv, hsend, hrecv, h0send, h0recv,
     csend, crecv, gsend, grecv, osend, orecv, oload,
 ):
@@ -142,6 +143,13 @@
         cp.start()
         return cp
 
+    def swap(n, s):
+        return [
+            send(disp_h.at[2 * other + s], prim_v.at[0, s, body_rows, own_cols], csend.at[n], crecv.at[n], peer_core),
+            send(cap_h.at[2 * other + s], a_v.at[s, :, own_cols], csend.at[n + 1], crecv.at[n + 1], peer_core),
+            send(cost_h.at[2 * other + s], cost_v.at[s, :, own_cols], csend.at[n + 2], crecv.at[n + 2], peer_core),
+        ]
+
     first = []
     for d in order + [0]:
         for cross in (0, 1):
@@ -152,6 +160,9 @@
                 p0s_v.at[other if cross else core], p0r_v.at[core, h_at],
                 p0send.at[cross, d], p0recv.at[cross, d], peer,
             ))
+        if d == order[0]:
+            swap_m = send(ml_v, m_v.at[:, own_cols], csend.at[0], crecv.at[0], peer_core)
+            swap_s = [swap(2, 0)]
     start_halo = []
     for side, to in ((0, left), (1, right)):
         for cross in (0, 1):
@@ -161,66 +172,54 @@
                 h0s_v.at[side, pair], h0r_v.at[1 - side, core],
                 h0send.at[side, cross], h0recv.at[side, cross], peer,
             ))
-    swaps = [
-        send(ml_v, m_v.at[:, own_cols], csend.at[0], crecv.at[0], peer_core),
-        send(fold_v.at[other], frecv_v, csend.at[1], crecv.at[1], peer_core),
-        send(disp_h.at[oth_pair], prim_v.at[0, :, body_rows, own_cols], csend.at[2], crecv.at[2], peer_core),
-        send(cap_h.at[oth_pair], a_v.at[:, :, own_cols], csend.at[3], crecv.at[3], peer_core),
-        send(cost_h.at[oth_pair], cost_v.at[:, :, own_cols], csend.at[4], crecv.at[4], peer_core),
-    ]
-    weights = send(wn_v, wnr_v, csend.at[5], crecv.at[5], peer_o0)
+    swap_s.append(swap(5, 1))
+    swap_f = send(fold_v.at[other], frecv_v, csend.at[1], crecv.at[1], peer_core)
+    weights = send(wn_v, wnr_v, csend.at[8], crecv.at[8], peer_o0)
     c_ml = load(14, ml_v, m_v.at[:, own_cols])
 
+    sb_v[...] = jnp.zeros_like(sb_v)
     c_ml.wait()
-    swaps[0].wait()
+    swap_m.wait()
     for j in range(4):
         mt_v[256 * j:256 * (j + 1), :] = m_v[:, 256 * j:256 * (j + 1)].T
-    swaps[1].wait()
-    for s in range(2):
-        for g in range(3):
-            for n, dest in ((0, invs_v), (1, base_v)):
-                mine, its = fold_v[core, n, s, g], frecv_v[n, s, g]
-                dest[s, g] = jnp.concatenate(
-                    [jnp.where(core == 0, mine, its), jnp.where(core == 0, its, mine)], axis=0
-                )
-    sb_v[...] = jnp.zeros_like(sb_v)
-    weights.wait()
-
-    def row_of(s, g):
-        ref = wn_v if s < 4 else wnr_v
-        at = 4 * (s % 4) + g
-        return ref[at:at + 1, :]
-
-    for g in range(3):
-        nodes = [row_of(s, g) for s in range(8)]
-        for s in range(4):
-            parts = [jnp.where(nodes[t] == nodes[s], row_of(t, 3), 0.0) for t in range(8)]
-            mass = ((parts[0] + parts[1]) + (parts[2] + parts[3])) + ((parts[4] + parts[5]) + (parts[6] + parts[7]))
-            scale = 1.0 / (mass + jnp.where(mass <= 0.0, 1.0, 0.0))
-            for t in range(8):
-                at = (3 * s + g) * 8 + t
-                co_v[at:at + 1, :] = parts[t] * scale
-
-    for cp in start_halo:
-        cp.wait()
-    c_disp.wait()
-    swaps[2].wait()
     keep_left = jnp.where(h_at > 0, 1.0, 0.0).astype(F32)
     keep_right = jnp.where(h_at < NH - 1, 1.0, 0.0).astype(F32)
-    for s in range(2):
-        for src in range(2):
-            lanes = slice(COLS_CORE * src, COLS_CORE * (src + 1))
-            prim_v[0, s, PAD - 1:PAD, lanes] = h0r_v[0, src, s] * keep_left
-            prim_v[0, s, PAD + HOURS_LOCAL:PAD + HOURS_LOCAL + 1, lanes] = h0r_v[1, src, s] * keep_right
+    c_disp.wait()
     c_a.wait()
-    swaps[3].wait()
     c_cost.wait()
-    swaps[4].wait()
     c_dual.wait()
     c_dem.wait()
 
+    def prepare():
+        swap_f.wait()
+        for s in range(2):
+            for g in range(3):
+                for n, dest in ((0, invs_v), (1, base_v)):
+                    mine, its = fold_v[core, n, s, g], frecv_v[n, s, g]
+                    dest[s, g] = jnp.concatenate(
+                        [jnp.where(core == 0, mine, its), jnp.where(core == 0, its, mine)], axis=0
+                    )
+
+    def coefficients():
+        weights.wait()
+
+        def row_of(s, g):
+            ref = wn_v if s < 4 else wnr_v
+            at = 4 * (s % 4) + g
+            return ref[at:at + 1, :]
+
+        for g in range(3):
+            nodes = [row_of(s, g) for s in range(8)]
+            for s in range(4):
+                parts = [jnp.where(nodes[t] == nodes[s], row_of(t, 3), 0.0) for t in range(8)]
+                mass = ((parts[0] + parts[1]) + (parts[2] + parts[3])) + ((parts[4] + parts[5]) + (parts[6] + parts[7]))
+                scale = 1.0 / (mass + jnp.where(mass <= 0.0, 1.0, 0.0))
+                for t in range(8):
+                    at = (3 * s + g) * 8 + t
+                    co_v[at:at + 1, :] = parts[t] * scale
+
     def image_copy(slot, s, half):
-        rows = pl.ds(2 * HALVES[half][0], 2 * HALVES[half][1])
+        rows = pl.ds(*SENT[half])
         return pltpu.make_async_remote_copy(
             src_ref=xs_v.at[s, rows], dst_ref=xr_v.at[slot, s, rows],
             send_sem=xsend.at[s, half], recv_sem=xrecv.at[slot, s, half],
@@ -241,71 +240,103 @@
             device_id=(s_at, hour_rel(d), r_at), device_id_type=MESH,
         )
 
+    def rows_of(ref, s, half, cols=slice(None)):
+        parts = [ref[s, r0:r0 + n, cols] for r0, n in PARTS[half]]
+        return parts[0] if len(parts) == 1 else jnp.concatenate(parts, axis=0)
+
+    def put_rows(ref, s, half, value):
+        at = 0
+        for r0, n in PARTS[half]:
+            ref[s, r0:r0 + n, :] = value[at:at + n]
+            at += n
+
     def dual_update(last, s, half):
-        r0, n = HALVES[half]
-        rows = pl.ds(r0, n)
         image_copy(last, s, half).wait_recv()
-        got = xr_v[last, s, 2 * r0:2 * (r0 + n), :].astype(F32)
-        got = jnp.concatenate([got[:n], got[n:]], axis=1)
-        pre_v[s, rows, :] = jnp.maximum(pre_v[s, rows, :] - STEP_DUAL * got, 0.0)
+        at, m = SENT[half]
+        got = xr_v[last, s, at:at + m, :].astype(F32)
+        got = jnp.concatenate([got[:m // 2], got[m // 2:]], axis=1)
+        put_rows(pre_v, s, half, jnp.maximum(rows_of(pre_v, s, half) - STEP_DUAL * got, 0.0))
 
     def chunk(k, now, s, half):
-        r0, n = HALVES[half]
         nxt = 1 - now
 
         @pl.when(k > 0)
         def _():
             dual_update(nxt, s, half)
-            side = half
-            halo_copy(now, 1 - side, s).wait_recv()
-            if half == 0:
+
+        if half == 0:
+            @pl.when(k > 0)
+            def _():
+                for side in range(2):
+                    halo_copy(now, side, s).wait_recv()
                 prim_v[now, s, PAD - 1:PAD, :] = hr_v[now, 0, s] * keep_left
-            else:
                 prim_v[now, s, PAD + HOURS_LOCAL:PAD + HOURS_LOCAL + 1, :] = hr_v[now, 1, s] * keep_right
 
-        dual = pre_v[s, r0:r0 + n, :]
+            @pl.when(k == 0)
+            def _():
+                if s == 0:
+                    for cp in start_halo:
+                        cp.wait()
+                for src in range(2):
+                    lanes = slice(COLS_CORE * src, COLS_CORE * (src + 1))
+                    prim_v[0, s, PAD - 1:PAD, lanes] = h0r_v[0, src, s] * keep_left
+                    prim_v[0, s, PAD + HOURS_LOCAL:PAD + HOURS_LOCAL + 1, lanes] = h0r_v[1, src, s] * keep_right
+        else:
+            @pl.when(k == 0)
+            def _():
+                for cp in swap_s[s]:
+                    cp.wait()
+
+        dual = rows_of(pre_v, s, half)
         low = dual.astype(BF16)
         image = None
         for j in range(4):
             cols = slice(256 * j, 256 * (j + 1))
-            pulled = jnp.dot(low, m_v[:, cols], preferred_element_type=F32)
-            p = prim_v[now, s, PAD + r0:PAD + r0 + n, cols]
-            up = prim_v[now, s, PAD + r0 - 1:PAD + r0 + n - 1, cols]
-            down = prim_v[now, s, PAD + r0 + 1:PAD + r0 + n + 1, cols]
+            pulled_all = jnp.dot(low, m_v[:, cols], preferred_element_type=F32)
             sb = jnp.concatenate([sb_v[s, 2 * j:2 * j + 1, :], sb_v[s, 2 * j + 1:2 * j + 2, :]], axis=1)
-            cap = jnp.maximum(a_v[s, r0:r0 + n, cols] - sb, 0.0)
-            rest = (cost_v[s, r0:r0 + n, cols] - pulled) + cap
-            fresh = (
-                (1.0 - 2.0 * RAMP_WEIGHT * STEP_PRIMAL) * p
-                + (RAMP_WEIGHT * STEP_PRIMAL) * (up + down)
-                - STEP_PRIMAL * rest
-            )
-            fresh = jnp.maximum(fresh, 0.0)
-            ext = 2.0 * fresh - p
-            prim_v[nxt, s, PAD + r0:PAD + r0 + n, cols] = fresh
-            a_v[s, r0:r0 + n, cols] = cap + STEP_CAP * ext
-            part = jnp.dot(ext.astype(BF16), mt_v[cols, :], preferred_element_type=F32)
+            exts = []
+            at = 0
+            for r0, n in PARTS[half]:
+                pulled = pulled_all[at:at + n]
+                at += n
+                p = prim_v[now, s, PAD + r0:PAD + r0 + n, cols]
+                up = prim_v[now, s, PAD + r0 - 1:PAD + r0 + n - 1, cols]
+                down = prim_v[now, s, PAD + r0 + 1:PAD + r0 + n + 1, cols]
+                cap = jnp.maximum(a_v[s, r0:r0 + n, cols] - sb, 0.0)
+                rest = (cost_v[s, r0:r0 + n, cols] - pulled) + cap
+                fresh = (
+                    (1.0 - 2.0 * RAMP_WEIGHT * STEP_PRIMAL) * p
+                    + (RAMP_WEIGHT * STEP_PRIMAL) * (up + down)
+                    - STEP_PRIMAL * rest
+                )
+                fresh = jnp.maximum(fresh, 0.0)
+                ext = 2.0 * fresh - p
+                prim_v[nxt, s, PAD + r0:PAD + r0 + n, cols] = fresh
+                a_v[s, r0:r0 + n, cols] = cap + STEP_CAP * ext
+                exts.append(ext)
+            ext_all = exts[0] if len(exts) == 1 else jnp.concatenate(exts, axis=0)
+            part = jnp.dot(ext_all.astype(BF16), mt_v[cols, :], preferred_element_type=F32)
             image = part if image is None else image + part
 
+        if half == 0:
+            @pl.when(k < ITERS - 1)
+            def _():
+                for side, row in ((0, PAD), (1, PAD + HOURS_LOCAL - 1)):
+                    @pl.when(k > 0)
+                    def _():
+                        halo_copy(nxt, side, s).wait_send()
+
+                    he_v[side, s] = prim_v[nxt, s, row:row + 1, :]
+                    halo_copy(nxt, side, s).start()
+
         @pl.when(k > 0)
         def _():
             image_copy(now, s, half).wait_send()
 
-        xs_v[s, 2 * r0:2 * (r0 + n), :] = jnp.concatenate([image[:, :128], image[:, 128:]], axis=0).astype(BF16)
+        at, m = SENT[half]
+        xs_v[s, at:at + m, :] = jnp.concatenate([image[:, :128], image[:, 128:]], axis=0).astype(BF16)
         image_copy(now, s, half).start()
-        pre_v[s, r0:r0 + n, :] = dual + STEP_DUAL * (dem_v[s, r0:r0 + n, :] - image)
-
-        @pl.when(k < ITERS - 1)
-        def _():
-            side = half
-
-            @pl.when(k > 0)
-            def _():
-                halo_copy(nxt, side, s).wait_send()
-
-            row = PAD if half == 0 else PAD + HOURS_LOCAL - 1
-            he_v[side, s] = prim_v[nxt, s, row:row + 1, :]
-            halo_copy(nxt, side, s).start()
+        put_rows(pre_v, s, half, dual + STEP_DUAL * (rows_of(dem_v, s, half) - image))
 
     def invest_step(total, s):
         mean = total * (1.0 / (NH * HOURS_LOCAL))
@@ -322,6 +353,7 @@
     def sums_in(k, now):
         @pl.when(k == 0)
         def _():
+            prepare()
             for cp in first:
                 cp.wait()
             for s in range(2):
@@ -335,21 +367,19 @@
 
         @pl.when(k > 0)
         def _():
-            for d in order:
-                sum_copy(now, d).wait_send()
             for d in order[::-1]:
                 sum_copy(now, d).wait_recv()
+            parts = [pr_v[now, h].astype(F32) for h in range(NH)]
+            while len(parts) > 1:
+                parts = [parts[i] + parts[i + 1] for i in range(0, len(parts), 2)]
             for s in range(2):
-                parts = [pr_v[now, h, s] for h in range(NH)]
-                while len(parts) > 1:
-                    parts = [parts[i] + parts[i + 1] for i in range(0, len(parts), 2)]
-                invest_step(parts[0], s)
+                invest_step(parts[0][8 * s:8 * (s + 1)], s)
 
     def step(k, carry):
         now = lax.rem(k, 2)
         nxt = 1 - now
         for s in range(2):
-            for half in range(2):
+            for half in (1, 0):
                 chunk(k, now, s, half)
         sums_in(k, now)
 
@@ -358,9 +388,20 @@
             for s in range(2):
                 for j in range(8):
                     left_over = jnp.maximum(a_v[s, :, 128 * j:128 * (j + 1)] - sb_v[s, j:j + 1, :], 0.0)
-                    pr_v[nxt, h_at, s, j:j + 1, :] = jnp.sum(left_over, axis=0, keepdims=True)
+                    at = 8 * s + j
+                    sum_v[at:at + 1, :] = jnp.sum(left_over, axis=0, keepdims=True)
+            pr_v[nxt, h_at] = sum_v[...].astype(BF16)
             for d in order:
                 sum_copy(nxt, d).start()
+
+        @pl.when(k > 0)
+        def _():
+            for d in order:
+                sum_copy(now, d).wait_send()
+
+        @pl.when(k == 0)
+        def _():
+            coefficients()
 
         @pl.when(k == ITERS - 1)
         def _():
@@ -426,6 +467,20 @@
     c_dual_own.wait()
 
 
+def hand_over(disp_i, dual_i, inv_i, mult_i, disp_o, dual_o, inv_o, mult_o, sem):
+    copies = []
+    pairs = [(inv_i, inv_o), (mult_i, mult_o)]
+    for s in range(4):
+        pairs.append((disp_i.at[s], disp_o.at[s]))
+    pairs.append((dual_i, dual_o))
+    for n, (src, dst) in enumerate(pairs):
+        copies.append(pltpu.make_async_copy(src, dst, sem.at[n]))
+    for cp in copies:
+        cp.start()
+    for cp in copies:
+        cp.wait()
+
+
 def shards(*args):
     args = args[:8] + tuple(jnp.transpose(x, (1, 0, 2)) for x in args[8:11]) + args[11:]
     hbm = pl.BlockSpec(memory_space=pltpu.HBM)
@@ -434,13 +489,13 @@
     disp, dual, inv, mult = pl.pallas_call(
         kernel,
         out_shape=(
-            jax.ShapeDtypeStruct((4, HOURS_LOCAL, COLS_CORE), F32),
-            jax.ShapeDtypeStruct((4, 64, HOURS_LOCAL), F32),
-            jax.ShapeDtypeStruct((3, 4, COLS_CORE), F32),
-            jax.ShapeDtypeStruct((3, 4, COLS_CORE), F32),
+            pltpu.VMEM((4, HOURS_LOCAL, COLS_CORE), F32),
+            pltpu.VMEM((4, 64, HOURS_LOCAL), F32),
+            pltpu.VMEM((3, 4, COLS_CORE), F32),
+            pltpu.VMEM((3, 4, COLS_CORE), F32),
         ),
         in_specs=[hbm] * 13,
-        out_specs=(hbm, hbm, vmem, vmem),
+        out_specs=(vmem,) * 4,
         scratch_shapes=[
             pltpu.VMEM((2, HOURS_LOCAL, COLS), F32),
             pltpu.VMEM((2, 2, HOURS_LOCAL + 2 * PAD, COLS), F32),
@@ -455,7 +510,7 @@
             pltpu.VMEM((2, HOURS_LOCAL, CONS), F32),
             pltpu.VMEM((2, 2 * HOURS_LOCAL, 128), BF16),
             pltpu.VMEM((2, 2, 2 * HOURS_LOCAL, 128), BF16),
-            pltpu.VMEM((2, NH, 2, 8, 128), F32),
+            pltpu.VMEM((2, NH, 16, 128), BF16),
             pltpu.VMEM((2, 2, 4, 128), F32),
             pltpu.VMEM((2, NH, 2, 4, 128), F32),
             pltpu.VMEM((2, 2, 1, COLS), F32),
@@ -476,6 +531,7 @@
             pltpu.VMEM((2, 2, 2, 3, 8, 128), F32),
             pltpu.VMEM((2, 12, 8, 128), F32),
             pltpu.VMEM((2, 2, 64, HOURS_LOCAL), F32),
+            pltpu.VMEM((16, 128), F32),
             pltpu.SMEM((4,), F32),
             pltpu.SMEM((3, 4), jnp.int32),
             dma((17,)),
@@ -484,7 +540,7 @@
             dma((2, NH)), dma((2, NH)),
             dma((2, 2)), dma((2, 2, 2)),
             dma((2, 2)), dma((2, 2)),
-            dma((6,)), dma((6,)),
+            dma((9,)), dma((9,)),
             dma((3,)), dma((3,)),
             dma((2,)), dma((2,)), dma((2,)),
         ],
@@ -493,6 +549,15 @@
         ),
         cost_estimate=pl.CostEstimate(flops=3 * 10**9, bytes_accessed=9 * 10**6, transcendentals=0),
     )(*args)
+    disp, dual, inv, mult = pl.pallas_call(
+        hand_over,
+        out_shape=tuple(jax.ShapeDtypeStruct(x.shape, x.dtype) for x in (disp, dual, inv, mult)),
+        in_specs=[vmem] * 4,
+        out_specs=(hbm,) * 4,
+        scratch_shapes=[dma((7,))],
+        compiler_params=pltpu.CompilerParams(vmem_limit_bytes=2**20),
+        cost_estimate=pl.CostEstimate(flops=0, bytes_accessed=3 * 10**6, transcendentals=0),
+    )(disp, dual, inv, mult)
     return disp, jnp.transpose(dual, (0, 2, 1)), jnp.transpose(inv, (1, 0, 2)), jnp.transpose(mult, (1, 0, 2))
 
 

time: 63.6 us -> 57.5 us (0.904)
  local copies, waits for them, and re-layouts: 4.49 us -> 0 us
  Pallas kernels: 58.3 us -> 56.7 us
    unnamed x10 -> x0, local copies, waits for them, and re-layouts: 4.49 us -> none
    pallas_call x1 -> x2, Pallas kernels: 58.3 us -> 56.7 us  [the longest x1 55.5 us: shards(): pl.pallas_call(kernel, out_shape=(pltpu.VMEM((4, HOURS_LOCAL, COLS_CORE),...]
where the time goes in v3:
time: 57.5 us; the launch traced here: 57.4 us
  Pallas kernels  56.7 us (99%)
  between operations  0.64 us (1%)
    pallas_call x1, Pallas kernels, shards(): pl.pallas_call(kernel, out_shape=(pltpu.VMEM((4, HOURS_LOCAL, COLS_CORE),...  55.5 us
    pallas_call x1, Pallas kernels, shards(): pl.pallas_call(hand_over, out_shape=tuple((jax.ShapeDtypeStruct(x.shape,...  1.24 us

profile of v3, /device:TPU:1, one launch (start us, length us, event | category | flops | bytes accessed | tf_op | source)
XLA Modules:
  0.0 57.4 jit_solution(12175613188872934886)
XLA Ops:
  0.6 55.5 %shard_map.156 = (f32[4,168,512]{2,1,0:T(8,128)S(1)}, f32[4,64,168]{2,1,0:T(8,128)S(1)}, f32[3,4,512]{2,1,0:T(4,128)S(1)}, f32[3,4,512]{2,1,0:T(4,128)S(1)}) custom-call(f32[4,168,512]{2,1,0:T(8,128)} %cost_h.1, f32[3,512]{1,0:T(4,128)} %icost_h.1, bf16[1,256,512]{2,1,0:T(8,128)(2,1)} %tile_h.1, s32[1,256,512]{2,1,0:T(8,128)} %mask_h.1, ...), custom_call_target="tpu_custom_call" | custom-call | flops 3000000000 | bytes 9000000 | tf_op jit(solution)/shard_map/pallas_call | solution.py:489
  56.1 1.2 %shard_map.157 = (f32[4,168,512]{2,1,0:T(8,128)}, f32[4,64,168]{2,1,0:T(8,128)}, f32[3,4,512]{2,1,0:T(4,128)}, f32[3,4,512]{2,1,0:T(4,128)}) custom-call(f32[4,168,512]{2,1,0:T(8,128)S(1)} %get-tuple-element.12.disp_i, f32[4,64,168]{2,1,0:T(8,128)S(1)} %get-tuple-element.13.dual_i, f32[3,4,512]{2,1,0:T(4,128)S(1)} %get-tuple-element.14.inv_i, ...), custom_call_target="tpu_custom_call" | custom-call | bytes 3000000 | tf_op jit(solution)/shard_map/pallas_call | solution.py:552

commit v4 on v3

--- a/solution.py
+++ b/solution.py
@@ -150,6 +150,15 @@
             send(cost_h.at[2 * other + s], cost_v.at[s, :, own_cols], csend.at[n + 2], crecv.at[n + 2], peer_core),
         ]
 
+    start_halo = []
+    for side, to in ((0, left), (1, right)):
+        for cross in (0, 1):
+            peer = (s_at, to, r_core if cross else r_at)
+            pair = oth_pair if cross else own_pair
+            start_halo.append(send(
+                h0s_v.at[side, pair], h0r_v.at[1 - side, core],
+                h0send.at[side, cross], h0recv.at[side, cross], peer,
+            ))
     first = []
     for d in order + [0]:
         for cross in (0, 1):
@@ -163,15 +172,6 @@
         if d == order[0]:
             swap_m = send(ml_v, m_v.at[:, own_cols], csend.at[0], crecv.at[0], peer_core)
             swap_s = [swap(2, 0)]
-    start_halo = []
-    for side, to in ((0, left), (1, right)):
-        for cross in (0, 1):
-            peer = (s_at, to, r_core if cross else r_at)
-            pair = oth_pair if cross else own_pair
-            start_halo.append(send(
-                h0s_v.at[side, pair], h0r_v.at[1 - side, core],
-                h0send.at[side, cross], h0recv.at[side, cross], peer,
-            ))
     swap_s.append(swap(5, 1))
     swap_f = send(fold_v.at[other], frecv_v, csend.at[1], crecv.at[1], peer_core)
     weights = send(wn_v, wnr_v, csend.at[8], crecv.at[8], peer_o0)
@@ -236,9 +236,13 @@
     def sum_copy(slot, d):
         return pltpu.make_async_remote_copy(
             src_ref=pr_v.at[slot, h_at], dst_ref=pr_v.at[slot, h_at],
-            send_sem=psend.at[slot, d], recv_sem=precv.at[slot, d],
+            send_sem=psend.at[slot], recv_sem=precv.at[slot],
             device_id=(s_at, hour_rel(d), r_at), device_id_type=MESH,
         )
+
+    def all_sums(slot, sem):
+        block = pr_v.at[slot, pl.ds(0, NH - 1)]
+        return pltpu.make_async_copy(block, block, sem.at[slot])
 
     def rows_of(ref, s, half, cols=slice(None)):
         parts = [ref[s, r0:r0 + n, cols] for r0, n in PARTS[half]]
@@ -367,8 +371,7 @@
 
         @pl.when(k > 0)
         def _():
-            for d in order[::-1]:
-                sum_copy(now, d).wait_recv()
+            all_sums(now, precv).wait()
             parts = [pr_v[now, h].astype(F32) for h in range(NH)]
             while len(parts) > 1:
                 parts = [parts[i] + parts[i + 1] for i in range(0, len(parts), 2)]
@@ -396,8 +399,7 @@
 
         @pl.when(k > 0)
         def _():
-            for d in order:
-                sum_copy(now, d).wait_send()
+            all_sums(now, psend).wait()
 
         @pl.when(k == 0)
         def _():
@@ -536,7 +538,7 @@
             pltpu.SMEM((3, 4), jnp.int32),
             dma((17,)),
             dma((2, 2)), dma((2, 2, 2)),
-            dma((2, NH)), dma((2, NH)),
+            dma((2,)), dma((2,)),
             dma((2, NH)), dma((2, NH)),
             dma((2, 2)), dma((2, 2, 2)),
             dma((2, 2)), dma((2, 2)),

time: 57.5 us -> 56.2 us (0.977)
  Pallas kernels: 56.7 us -> 55.4 us
    pallas_call x1, Pallas kernels: 55.5 us -> 54.2 us  [shards(): pl.pallas_call(kernel, out_shape=(pltpu.VMEM((4, HOURS_LOCAL, COLS_CORE),...]
where the time goes in v4:
time: 56.2 us; the launch traced here: 56.1 us
  Pallas kernels  55.4 us (99%)
  between operations  0.64 us (1%)
    pallas_call x1, Pallas kernels, shards(): pl.pallas_call(kernel, out_shape=(pltpu.VMEM((4, HOURS_LOCAL, COLS_CORE),...  54.2 us
    pallas_call x1, Pallas kernels, shards(): pl.pallas_call(hand_over, out_shape=tuple((jax.ShapeDtypeStruct(x.shape,...  1.24 us

profile of v4, /device:TPU:1, one launch (start us, length us, event | category | flops | bytes accessed | tf_op | source)
XLA Modules:
  0.0 56.1 jit_solution(6362955046215769405)
XLA Ops:
  0.6 54.2 %shard_map.156 = (f32[4,168,512]{2,1,0:T(8,128)S(1)}, f32[4,64,168]{2,1,0:T(8,128)S(1)}, f32[3,4,512]{2,1,0:T(4,128)S(1)}, f32[3,4,512]{2,1,0:T(4,128)S(1)}) custom-call(f32[4,168,512]{2,1,0:T(8,128)} %cost_h.1, f32[3,512]{1,0:T(4,128)} %icost_h.1, bf16[1,256,512]{2,1,0:T(8,128)(2,1)} %tile_h.1, s32[1,256,512]{2,1,0:T(8,128)} %mask_h.1, ...), custom_call_target="tpu_custom_call" | custom-call | flops 3000000000 | bytes 9000000 | tf_op jit(solution)/shard_map/pallas_call | solution.py:491
  54.8 1.2 %shard_map.157 = (f32[4,168,512]{2,1,0:T(8,128)}, f32[4,64,168]{2,1,0:T(8,128)}, f32[3,4,512]{2,1,0:T(4,128)}, f32[3,4,512]{2,1,0:T(4,128)}) custom-call(f32[4,168,512]{2,1,0:T(8,128)S(1)} %get-tuple-element.12.disp_i, f32[4,64,168]{2,1,0:T(8,128)S(1)} %get-tuple-element.13.dual_i, f32[3,4,512]{2,1,0:T(4,128)S(1)} %get-tuple-element.14.inv_i, ...), custom_call_target="tpu_custom_call" | custom-call | bytes 3000000 | tf_op jit(solution)/shard_map/pallas_call | solution.py:554

commit v5 on v4

--- a/solution.py
+++ b/solution.py
@@ -150,6 +150,8 @@
             send(cost_h.at[2 * other + s], cost_v.at[s, :, own_cols], csend.at[n + 2], crecv.at[n + 2], peer_core),
         ]
 
+    swap_m = send(ml_v, m_v.at[:, own_cols], csend.at[0], crecv.at[0], peer_core)
+    swap_s = [swap(2, 0), swap(5, 1)]
     start_halo = []
     for side, to in ((0, left), (1, right)):
         for cross in (0, 1):
@@ -169,10 +171,6 @@
                 p0s_v.at[other if cross else core], p0r_v.at[core, h_at],
                 p0send.at[cross, d], p0recv.at[cross, d], peer,
             ))
-        if d == order[0]:
-            swap_m = send(ml_v, m_v.at[:, own_cols], csend.at[0], crecv.at[0], peer_core)
-            swap_s = [swap(2, 0)]
-    swap_s.append(swap(5, 1))
     swap_f = send(fold_v.at[other], frecv_v, csend.at[1], crecv.at[1], peer_core)
     weights = send(wn_v, wnr_v, csend.at[8], crecv.at[8], peer_o0)
     c_ml = load(14, ml_v, m_v.at[:, own_cols])
@@ -354,40 +352,46 @@
             spent = ext if spent is None else spent + ext
         sb_v[s] = STEP_CAP * spent
 
+    def first_sums():
+        prepare()
+        for cp in first:
+            cp.wait()
+        for s in range(2):
+            parts = []
+            for src in range(2):
+                total = p0r_v[src, 0, s]
+                for h in range(1, NH):
+                    total = total + p0r_v[src, h, s]
+                parts.append(total)
+            invest_step(jnp.concatenate(parts, axis=0), s)
+
+    def later_sums(now):
+        all_sums(now, precv).wait()
+        parts = [pr_v[now, h].astype(F32) for h in range(NH)]
+        while len(parts) > 1:
+            parts = [parts[i] + parts[i + 1] for i in range(0, len(parts), 2)]
+        for s in range(2):
+            invest_step(parts[0][8 * s:8 * (s + 1)], s)
+
     def sums_in(k, now):
         @pl.when(k == 0)
         def _():
-            prepare()
-            for cp in first:
-                cp.wait()
-            for s in range(2):
-                parts = []
-                for src in range(2):
-                    total = p0r_v[src, 0, s]
-                    for h in range(1, NH):
-                        total = total + p0r_v[src, h, s]
-                    parts.append(total)
-                invest_step(jnp.concatenate(parts, axis=0), s)
+            first_sums()
 
         @pl.when(k > 0)
         def _():
-            all_sums(now, precv).wait()
-            parts = [pr_v[now, h].astype(F32) for h in range(NH)]
-            while len(parts) > 1:
-                parts = [parts[i] + parts[i + 1] for i in range(0, len(parts), 2)]
-            for s in range(2):
-                invest_step(parts[0][8 * s:8 * (s + 1)], s)
+            later_sums(now)
 
     def step(k, carry):
         now = lax.rem(k, 2)
         nxt = 1 - now
-        for s in range(2):
-            for half in (1, 0):
+        for half in (1, 0):
+            for s in range(2):
                 chunk(k, now, s, half)
-        sums_in(k, now)
 
         @pl.when(k < ITERS - 1)
         def _():
+            sums_in(k, now)
             for s in range(2):
                 for j in range(8):
                     left_over = jnp.maximum(a_v[s, :, 128 * j:128 * (j + 1)] - sb_v[s, j:j + 1, :], 0.0)
@@ -397,7 +401,7 @@
             for d in order:
                 sum_copy(nxt, d).start()
 
-        @pl.when(k > 0)
+        @pl.when((k > 0) & (k < ITERS - 1))
         def _():
             all_sums(now, psend).wait()
 
@@ -405,19 +409,10 @@
         def _():
             coefficients()
 
-        @pl.when(k == ITERS - 1)
-        def _():
-            g_v[0, core] = invs_v[...]
-
         return carry
 
     lax.fori_loop(0, ITERS, step, 0)
 
-    gathers = [
-        send(g_v.at[0, core], g_v.at[1, core], gsend.at[1], grecv.at[1], peer_o0),
-        send(g_v.at[0, core], g_v.at[1, core], gsend.at[2], grecv.at[2], peer_o1),
-        send(g_v.at[0, core], g_v.at[0, core], gsend.at[0], grecv.at[0], peer_core),
-    ]
     end = ITERS % 2
     outs = [
         send(
@@ -427,6 +422,15 @@
     ]
     c_own = pltpu.make_async_copy(prim_v.at[end, :, body_rows, own_cols], disp_o.at[own_pair], oload.at[0])
     c_own.start()
+
+    later_sums(1 - end)
+    g_v[0, core] = invs_v[...]
+    gathers = [
+        send(g_v.at[0, core], g_v.at[1, core], gsend.at[1], grecv.at[1], peer_o0),
+        send(g_v.at[0, core], g_v.at[1, core], gsend.at[2], grecv.at[2], peer_o1),
+        send(g_v.at[0, core], g_v.at[0, core], gsend.at[0], grecv.at[0], peer_core),
+    ]
+    all_sums(1 - end, psend).wait()
 
     on_first = jnp.where(r_at < 2, 1.0, 0.0).astype(F32) > 0.5
     for s in range(2):
@@ -445,23 +449,32 @@
         for s in range(2):
             halo_copy(end, side, s).wait_send()
 
-    for cp in gathers[::-1]:
-        cp.wait()
+    def share(group, s, g):
+        spread = None
+        for t in range(4 * group, 4 * group + 4):
+            at = (3 * s + g) * 8 + t
+            term = co_v[at:at + 1, :] * g_v[group, (t // 2) % 2, t % 2, g]
+            spread = term if spread is None else spread + term
+        return spread
+
+    gathers[2].wait()
     for g in range(3):
-        invs = [g_v[t // 4, (t // 2) % 2, t % 2, g] for t in range(8)]
         for s in range(4):
-            spread = None
-            for t in range(8):
-                at = (3 * s + g) * 8 + t
-                term = co_v[at:at + 1, :] * invs[t]
-                spread = term if spread is None else spread + term
-            tmp_v[0, 3 * s + g] = invs[s]
-            tmp_v[1, 3 * s + g] = PENALTY * (invs[s] - spread)
+            inv = g_v[0, s // 2, s % 2, g]
+            tmp_v[0, 3 * s + g] = inv
+            tmp_v[1, 3 * s + g] = inv - share(0, s, g)
     for s in range(4):
         for g in range(3):
             for i in range(4):
                 lanes = slice(128 * i, 128 * (i + 1))
                 inv_o[g, s:s + 1, lanes] = tmp_v[0, 3 * s + g, pl.ds(4 * core + i, 1), :]
+    gathers[1].wait()
+    gathers[0].wait()
+    for g in range(3):
+        for s in range(4):
+            tmp_v[1, 3 * s + g] = PENALTY * (tmp_v[1, 3 * s + g] - share(1, s, g))
+            for i in range(4):
+                lanes = slice(128 * i, 128 * (i + 1))
                 mult_o[g, s:s + 1, lanes] = il_v[1, g, s:s + 1, lanes] + tmp_v[1, 3 * s + g, pl.ds(4 * core + i, 1), :]
     for cp in outs:
         cp.wait()

time: 56.2 us -> 56.1 us (level)
  no operation moved by 1% of the time
where the time goes in v5:
time: 56.1 us; the launch traced here: 56 us
  Pallas kernels  55.4 us (99%)
  between operations  0.64 us (1%)
    pallas_call x1, Pallas kernels, shards(): pl.pallas_call(kernel, out_shape=(pltpu.VMEM((4, HOURS_LOCAL, COLS_CORE),...  54.1 us
    pallas_call x1, Pallas kernels, shards(): pl.pallas_call(hand_over, out_shape=tuple((jax.ShapeDtypeStruct(x.shape,...  1.24 us

profile of v5, /device:TPU:1, one launch (start us, length us, event | category | flops | bytes accessed | tf_op | source)
XLA Modules:
  0.0 56.0 jit_solution(2608619825859294701)
XLA Ops:
  0.6 54.1 %shard_map.156 = (f32[4,168,512]{2,1,0:T(8,128)S(1)}, f32[4,64,168]{2,1,0:T(8,128)S(1)}, f32[3,4,512]{2,1,0:T(4,128)S(1)}, f32[3,4,512]{2,1,0:T(4,128)S(1)}) custom-call(f32[4,168,512]{2,1,0:T(8,128)} %cost_h.1, f32[3,512]{1,0:T(4,128)} %icost_h.1, bf16[1,256,512]{2,1,0:T(8,128)(2,1)} %tile_h.1, s32[1,256,512]{2,1,0:T(8,128)} %mask_h.1, ...), custom_call_target="tpu_custom_call" | custom-call | flops 3000000000 | bytes 9000000 | tf_op jit(solution)/shard_map/pallas_call | solution.py:504
  54.8 1.2 %shard_map.157 = (f32[4,168,512]{2,1,0:T(8,128)}, f32[4,64,168]{2,1,0:T(8,128)}, f32[3,4,512]{2,1,0:T(4,128)}, f32[3,4,512]{2,1,0:T(4,128)}) custom-call(f32[4,168,512]{2,1,0:T(8,128)S(1)} %get-tuple-element.12.disp_i, f32[4,64,168]{2,1,0:T(8,128)S(1)} %get-tuple-element.13.dual_i, f32[3,4,512]{2,1,0:T(4,128)S(1)} %get-tuple-element.14.inv_i, ...), custom_call_target="tpu_custom_call" | custom-call | bytes 3000000 | tf_op jit(solution)/shard_map/pallas_call | solution.py:567

commit v6 on v4

--- a/solution.py
+++ b/solution.py
@@ -150,6 +150,9 @@
             send(cost_h.at[2 * other + s], cost_v.at[s, :, own_cols], csend.at[n + 2], crecv.at[n + 2], peer_core),
         ]
 
+    swap_m = send(ml_v, m_v.at[:, own_cols], csend.at[0], crecv.at[0], peer_core)
+    swap_f = send(fold_v.at[other], frecv_v, csend.at[1], crecv.at[1], peer_core)
+    swap_s = [swap(2, 0), swap(5, 1)]
     start_halo = []
     for side, to in ((0, left), (1, right)):
         for cross in (0, 1):
@@ -169,11 +172,6 @@
                 p0s_v.at[other if cross else core], p0r_v.at[core, h_at],
                 p0send.at[cross, d], p0recv.at[cross, d], peer,
             ))
-        if d == order[0]:
-            swap_m = send(ml_v, m_v.at[:, own_cols], csend.at[0], crecv.at[0], peer_core)
-            swap_s = [swap(2, 0)]
-    swap_s.append(swap(5, 1))
-    swap_f = send(fold_v.at[other], frecv_v, csend.at[1], crecv.at[1], peer_core)
     weights = send(wn_v, wnr_v, csend.at[8], crecv.at[8], peer_o0)
     c_ml = load(14, ml_v, m_v.at[:, own_cols])
 
@@ -357,7 +355,6 @@
     def sums_in(k, now):
         @pl.when(k == 0)
         def _():
-            prepare()
             for cp in first:
                 cp.wait()
             for s in range(2):
@@ -411,6 +408,7 @@
 
         return carry
 
+    prepare()
     lax.fori_loop(0, ITERS, step, 0)
 
     gathers = [

time: 56.2 us -> 56.3 us (level)
  no operation moved by 1% of the time
where the time goes in v6:
time: 56.3 us; the launch traced here: 56.2 us
  Pallas kernels  55.6 us (99%)
  between operations  0.64 us (1%)
    pallas_call x1, Pallas kernels, shards(): pl.pallas_call(kernel, out_shape=(pltpu.VMEM((4, HOURS_LOCAL, COLS_CORE),...  54.4 us
    pallas_call x1, Pallas kernels, shards(): pl.pallas_call(hand_over, out_shape=tuple((jax.ShapeDtypeStruct(x.shape,...  1.24 us

profile of v6, /device:TPU:1, one launch (start us, length us, event | category | flops | bytes accessed | tf_op | source)
XLA Modules:
  0.0 56.2 jit_solution(11375597345299209682)
XLA Ops:
  0.6 54.4 %shard_map.156 = (f32[4,168,512]{2,1,0:T(8,128)S(1)}, f32[4,64,168]{2,1,0:T(8,128)S(1)}, f32[3,4,512]{2,1,0:T(4,128)S(1)}, f32[3,4,512]{2,1,0:T(4,128)S(1)}) custom-call(f32[4,168,512]{2,1,0:T(8,128)} %cost_h.1, f32[3,512]{1,0:T(4,128)} %icost_h.1, bf16[1,256,512]{2,1,0:T(8,128)(2,1)} %tile_h.1, s32[1,256,512]{2,1,0:T(8,128)} %mask_h.1, ...), custom_call_target="tpu_custom_call" | custom-call | flops 3000000000 | bytes 9000000 | tf_op jit(solution)/shard_map/pallas_call | solution.py:489
  55.0 1.2 %shard_map.157 = (f32[4,168,512]{2,1,0:T(8,128)}, f32[4,64,168]{2,1,0:T(8,128)}, f32[3,4,512]{2,1,0:T(4,128)}, f32[3,4,512]{2,1,0:T(4,128)}) custom-call(f32[4,168,512]{2,1,0:T(8,128)S(1)} %get-tuple-element.12.disp_i, f32[4,64,168]{2,1,0:T(8,128)S(1)} %get-tuple-element.13.dual_i, f32[3,4,512]{2,1,0:T(4,128)S(1)} %get-tuple-element.14.inv_i, ...), custom_call_target="tpu_custom_call" | custom-call | bytes 3000000 | tf_op jit(solution)/shard_map/pallas_call | solution.py:552
